TPU v7x, 512 devices: a whole 4x8x8 slice. The times are simulated.
512 devices in a mesh: dp: 32 (over z, x), expert: 16 (over y, core).
Axes of the slice: x: 4, y: 8, z: 8, core: 2. Of those that a mesh axis runs over, the one named last changes fastest.
Arguments:
- tokens: bfloat16 [1024, 3072], P(('dp', 'expert')), may hold values from -6 to 6
- cotangent: bfloat16 [1024, 3072], P(('dp', 'expert')), may hold values from -6 to 6
- route_ids: int32 [1024, 4], P(('dp', 'expert')), may hold values from 0 to 15, all different within a row; in each aligned block of 32 rows (0 to 31, 32 to 63, ...) at most 16 rows name the same one
- gate_probs: float32 [1024, 4], P(('dp', 'expert')), may hold values from 0.05 to 1
- w_gate: bfloat16 [16, 3072, 5376], P('expert', None, 'dp'), may hold values from -0.109375 to 0.109375
- w_up: bfloat16 [16, 3072, 5376], P('expert', None, 'dp'), may hold values from -0.109375 to 0.109375
- w_down: bfloat16 [16, 5376, 3072], P('expert', 'dp'), may hold values from -0.078125 to 0.078125
Outputs:
- token_grad: bfloat16 [1024, 3072], P(('dp', 'expert'))
- down_grad: bfloat16 [16, 5376, 3072], P('expert', 'dp')
Inputs may be any that keep to these rules, and one draw needn't show every extreme that they name: `route_ids`: each row names 4 different experts. In each aligned block of 32 rows (the tokens of one index of dp) no expert is named by more than 16 rows, a bound that some block reaches.
All inputs are finite; a program needn't handle non-finite values.
Results may differ from a plain program's by a relative error of at most 0.023.
Values may be sent and summed in bfloat16 or wider, within the bound.
A program may use at most 64 MiB of HBM per device.

v0:
```python
import jax
import jax.numpy as jnp
from jax import lax
from jax.sharding import PartitionSpec as P


def silu_parts(gate_pre):
    sigma = jax.nn.sigmoid(gate_pre)
    return (gate_pre * sigma, sigma * (1.0 + gate_pre * (1.0 - sigma)))


def backward_rows(gate_pre, up_pre, grad_piece, down_local):
    active, slope_term = silu_parts(gate_pre)
    hidden = (active * up_pre).astype(jnp.bfloat16)
    hidden_grad = lax.dot_general(
        grad_piece, down_local, (((1,), (1,)), ((), ())), preferred_element_type=jnp.float32
    )
    gate_grad = (hidden_grad * up_pre * slope_term).astype(jnp.bfloat16)
    up_grad = (hidden_grad * active).astype(jnp.bfloat16)
    down_part = lax.dot_general(
        hidden, grad_piece, (((0,), (0,)), ((), ())), preferred_element_type=jnp.float32
    )
    return (down_part, jnp.concatenate([gate_grad, up_grad], axis=1))


def on_device(tokens, cotangent, route_ids, gate_probs, w_gate, w_up, w_down):
    expert_count = lax.axis_size("expert")
    token_count, model_width = tokens.shape
    choices_per = route_ids.shape[1]
    gate_local = w_gate[0]
    up_local = w_up[0]
    down_local = w_down[0]
    hidden_local = gate_local.shape[1]
    matches = route_ids[:, :, None] == jnp.arange(expert_count, dtype=jnp.int32)[None, None, :]
    routed = jnp.sum(matches.astype(jnp.float32), axis=1)
    weights = jnp.sum(jnp.where(matches, gate_probs[:, :, None], 0.0), axis=1)
    send_tokens = tokens[None, :, :] * routed.T[:, :, None].astype(jnp.bfloat16)
    send_grads = (weights.T[:, :, None] * cotangent[None, :, :].astype(jnp.float32)).astype(
        jnp.bfloat16
    )
    occupied = routed.T.astype(jnp.int32)
    recv_tokens, recv_grads, recv_occupied = (
        lax.all_to_all(send_tokens, "expert", split_axis=0, concat_axis=0, tiled=True),
        lax.all_to_all(send_grads, "expert", split_axis=0, concat_axis=0, tiled=True),
        lax.all_to_all(occupied, "expert", split_axis=0, concat_axis=0, tiled=True),
    )
    slot_count = expert_count * token_count
    flat_tokens = recv_tokens.reshape(slot_count, model_width)
    flat_grads = recv_grads.reshape(slot_count, model_width)
    most_rows = min(token_count * expert_count, 2 * token_count * choices_per)
    flags = recv_occupied.reshape(slot_count)
    position = jnp.cumsum(flags) - 1
    placing = (
        (position[None, :] == jnp.arange(most_rows, dtype=jnp.int32)[:, None])
        & (flags[None, :] > 0)
    ).astype(jnp.bfloat16)
    rows_tok = jnp.dot(placing, flat_tokens, preferred_element_type=jnp.float32).astype(
        jnp.bfloat16
    )
    rows_grad = jnp.dot(placing, flat_grads, preferred_element_type=jnp.float32).astype(
        jnp.bfloat16
    )
    piece = (
        lax.all_gather(rows_tok, "dp", axis=0, tiled=True),
        lax.all_gather(rows_grad, "dp", axis=0, tiled=True),
    )
    gate_pre = jnp.dot(piece[0], gate_local, preferred_element_type=jnp.float32)
    up_pre = jnp.dot(piece[0], up_local, preferred_element_type=jnp.float32)
    down_part, pair_rows = backward_rows(gate_pre, up_pre, piece[1], down_local)
    term = lax.dot_general(
        pair_rows[:, :hidden_local],
        gate_local,
        (((1,), (1,)), ((), ())),
        preferred_element_type=jnp.float32,
    )
    summed = lax.psum_scatter(
        (
            term
            + lax.dot_general(
                pair_rows[:, hidden_local:],
                up_local,
                (((1,), (1,)), ((), ())),
                preferred_element_type=jnp.float32,
            )
        ).astype(jnp.bfloat16),
        "dp",
        scatter_dimension=0,
        tiled=True,
    )
    spread = jnp.dot(placing.T, summed, preferred_element_type=jnp.float32).astype(jnp.bfloat16)
    returned = lax.all_to_all(
        spread.reshape(expert_count, token_count, model_width),
        "expert",
        split_axis=0,
        concat_axis=0,
        tiled=True,
    )
    token_grad = jnp.sum(returned.astype(jnp.float32), axis=0).astype(jnp.bfloat16)
    return (token_grad, down_part.astype(jnp.bfloat16)[None])


def solution(mesh):
    in_specs = (
        P(("dp", "expert"), None),
        P(("dp", "expert"), None),
        P(("dp", "expert"), None),
        P(("dp", "expert"), None),
        P("expert", None, "dp"),
        P("expert", None, "dp"),
        P("expert", "dp", None),
    )
    out_specs = (P(("dp", "expert"), None), P("expert", "dp", None))
    return jax.shard_map(
        on_device, mesh=mesh, in_specs=in_specs, out_specs=out_specs, check_vma=False
    )
```

profile of v0, /device:TPU:6, one launch (start us, length us, event | category | flops | bytes accessed | tf_op | source)
XLA Modules:
  0.0 464.5 jit_solution(3701283448048248844)
XLA Ops:
  7.2 0.9 select_reduce_fusion
  8.7 7.2 %all-to-all-start = ((s32[16,1,2]{2,1,0:T(1,128)}), s32[16,1,2]{2,1,0:T(1,128)S(1)}, u32[]{:S(2)}, u32[]{:S(2)}) async-start(s32[16,1,2]{2,1,0:T(1,128)} %copy.23), calls=%async_computation | async-start | bytes 16384 | tf_op jit(solution)/shard_map/all_to_all | solution.py:45
  16.0 1.6 broadcast_multiply_fusion
  17.6 5.8 %all-to-all-done = s32[16,1,2]{2,1,0:T(1,128)S(1)} async-done(((s32[16,1,2]{2,1,0:T(1,128)}), s32[16,1,2]{2,1,0:T(1,128)S(1)}, u32[]{:S(2)}, u32[]{:S(2)}) %all-to-all-start) | async-done | bytes 160 | tf_op jit(solution)/shard_map/all_to_all | solution.py:45
  23.5 3.5 all-to-all-start.2
  28.6 8.2 %all-to-all-done.2 = bf16[16,2,3072]{2,1,0:T(2,128)(2,1)S(1)} async-done(((bf16[16,2,3072]{2,1,0:T(2,128)(2,1)}), bf16[16,2,3072]{2,1,0:T(2,128)(2,1)S(1)}, u32[]{:S(2)}, u32[]{:S(2)}) %all-to-all-start.2) | async-done | bytes 196640 | tf_op jit(solution)/shard_map/all_to_all | solution.py:43
  36.9 0.8 convolution_convert_fusion.2
  37.9 0.8 convert_element_type.53
  38.9 13.0 %all_to_all.24 = bf16[16,2,3072]{2,1,0:T(2,128)(2,1)S(1)} all-to-all(bf16[16,2,3072]{2,1,0:T(2,128)(2,1)S(1)} %multiply_convert_fusion), channel_id=1, replica_groups=mesh['dp'=32,'expert'=16] {'expert'}, dimensions={0} | all-to-all | bytes 393216 | tf_op jit(solution)/shard_map/all_to_all | solution.py:44
  52.0 0.8 convolution_convert_fusion.3
  52.8 70.5 %all-gather.5.cloned.1.call-done = bf16[512,3072]{1,0:T(8,128)(2,1)} async-done(((bf16[16,3072]{1,0:T(8,128)(2,1)}), bf16[512,3072]{1,0:T(8,128)(2,1)}) %all-gather.5.cloned.1.call-update) | async-done | bytes 3145744 | tf_op jit(solution)/shard_map/all_gather | solution.py:64
  123.3 3.2 fusion.3
  126.6 1.2 fusion.6
  127.8 81.0 %all-gather.3.cloned.1.call-done = bf16[512,3072]{1,0:T(8,128)(2,1)} async-done(((bf16[16,3072]{1,0:T(8,128)(2,1)}), bf16[512,3072]{1,0:T(8,128)(2,1)}) %all-gather.3.cloned.1.call-update) | async-done | bytes 3145744 | tf_op jit(solution)/shard_map/all_gather | solution.py:65
  208.8 3.4 fusion.8
  212.1 1.1 fusion.1
  213.2 2.8 add_convert_fusion
  216.1 222.4 %reduce-scatter.2.cloned.1.call-done = bf16[16,3072]{1,0:T(8,128)(2,1)} async-done(((bf16[512,3072]{1,0:T(8,128)(2,1)}), bf16[16,3072]{1,0:T(8,128)(2,1)}) %reduce-scatter.2.cloned.1.call-update) | async-done | bytes 98320 | tf_op jit(solution)/shard_map/reduce_scatter | solution.py:76
  438.4 1.1 convolution_convert_fusion.1
  439.6 0.8 reshape.66
  440.4 6.9 %all-to-all-start.3 = ((bf16[16,2,3072]{2,1,0:T(2,128)(2,1)}), bf16[16,2,3072]{2,1,0:T(2,128)(2,1)S(1)}, u32[]{:S(2)}, u32[]{:S(2)}) async-start(bf16[16,2,3072]{2,1,0:T(2,128)(2,1)} %reshape.66), calls=%async_computation.4 | async-start | bytes 393216 | tf_op jit(solution)/shard_map/all_to_all | solution.py:91
  447.2 3.6 fusion
  450.8 6.4 %all-to-all-done.3 = bf16[16,2,3072]{2,1,0:T(2,128)(2,1)S(1)} async-done(((bf16[16,2,3072]{2,1,0:T(2,128)(2,1)}), bf16[16,2,3072]{2,1,0:T(2,128)(2,1)S(1)}, u32[]{:S(2)}, u32[]{:S(2)}) %all-to-all-start.3) | async-done | bytes 196640 | tf_op jit(solution)/shard_map/all_to_all | solution.py:91
  457.2 0.8 reduce_sum.32
  (26 shorter events, 3.0 us)
Async XLA Ops:
  7.2 116.2 %copy-start = (bf16[1,3072,168]{1,2,0:T(8,128)(2,1)S(1)}, bf16[1,3072,168]{1,2,0:T(8,128)(2,1)}, u32[]{:S(2)}) copy-start(bf16[1,3072,168]{1,2,0:T(8,128)(2,1)} %param.11) | copy-start | bytes 3096580
  8.7 14.7 %all-to-all-start = ((s32[16,1,2]{2,1,0:T(1,128)}), s32[16,1,2]{2,1,0:T(1,128)S(1)}, u32[]{:S(2)}, u32[]{:S(2)}) async-start(s32[16,1,2]{2,1,0:T(1,128)} %copy.23), calls=%async_computation | async-start | bytes 16384 | tf_op jit(solution)/shard_map/all_to_all | solution.py:45
  23.5 13.4 %all-to-all-start.2 = ((bf16[16,2,3072]{2,1,0:T(2,128)(2,1)}), bf16[16,2,3072]{2,1,0:T(2,128)(2,1)S(1)}, u32[]{:S(2)}, u32[]{:S(2)}) async-start(bf16[16,2,3072]{2,1,0:T(2,128)(2,1)} %broadcast_multiply_fusion), calls=%async_computation.2 | async-start | bytes 393216 | tf_op jit(solution)/shard_map/all_to_all | solution.py:43
  27.0 96.3 %all-gather.5.cloned.1.call-start = ((), (), s32[]{:S(2)}) async-start(), calls=%async_computation.6 | async-start | bytes 3244032 | tf_op jit(solution)/shard_map/all_gather | solution.py:64
  37.7 88.8 %copy-start.1 = (bf16[1,3072,168]{1,2,0:T(8,128)(2,1)S(1)}, bf16[1,3072,168]{1,2,0:T(8,128)(2,1)}, u32[]{:S(2)}) copy-start(bf16[1,3072,168]{1,2,0:T(8,128)(2,1)} %param.12) | copy-start | bytes 3096580
  37.7 171.0 %all-gather.3.cloned.1.call-start = ((), (), s32[]{:S(2)}) async-start(), calls=%async_computation.5 | async-start | bytes 3244032 | tf_op jit(solution)/shard_map/all_gather | solution.py:65
  52.8 385.7 %reduce-scatter.2.cloned.1.call-start = ((), (), s32[]{:S(2)}) async-start(), calls=%async_computation.7 | async-start | bytes 3244032 | tf_op jit(solution)/shard_map/reduce_scatter | solution.py:76
  123.3 3.2 copy-start.2
  440.4 16.8 %all-to-all-start.3 = ((bf16[16,2,3072]{2,1,0:T(2,128)(2,1)}), bf16[16,2,3072]{2,1,0:T(2,128)(2,1)S(1)}, u32[]{:S(2)}, u32[]{:S(2)}) async-start(bf16[16,2,3072]{2,1,0:T(2,128)(2,1)} %reshape.66), calls=%async_computation.4 | async-start | bytes 393216 | tf_op jit(solution)/shard_map/all_to_all | solution.py:91
Sparse Core Ops, SparseCore 0:
  37.8 85.4 all-gather.4
  126.5 82.2 all-gather.2
  216.2 222.2 reduce-scatter.1
where the time goes:
time: 468 us; the launch traced here: 464 us
  waiting for transfers between devices  394 us (84%)
  matrix products  18 us (4%)
  starting transfers between devices  17.7 us (4%)
  between operations  13.8 us (3%)
  blocking collectives  13 us (3%)
  other arithmetic  5.11 us (1%)
    reduce_scatter x1, waiting for transfers between devices, on_device(): lax.psum_scatter((term + lax.dot_general(pair_rows[:, hidden_local:], up_...  222 us
    all_gather x1, waiting for transfers between devices, on_device(): lax.all_gather(rows_grad, 'dp', axis=0, tiled=True)  81 us
    all_gather x1, waiting for transfers between devices, on_device(): lax.all_gather(rows_tok, 'dp', axis=0, tiled=True)  70.5 us
    all_to_all x1, blocking collectives, on_device(): lax.all_to_all(send_grads, 'expert', split_axis=0, concat_axis=0, tiled=T...  13 us
  transfers between devices with their start and end apart: 6, of which 6 were waited for; matrix products, arithmetic and copies ran while one was open for 3% of the time, Pallas kernels for 0%

commit v1 on v0

v1 whole, which is shorter than its diff:
```python
import functools

import jax
import jax.numpy as jnp
import numpy as np
from jax import lax
from jax.experimental import pallas as pl
from jax.experimental.pallas import tpu as pltpu
from jax.sharding import PartitionSpec as P

MESH = pl.DeviceIdType.MESH
F32 = jnp.float32
BF16 = jnp.bfloat16
PIECES = 3
ROWS = 16
LANES = 128
SEGS = 8
WIDE = SEGS * LANES
ORDERS = (("x", "y", "z"), ("y", "z", "x"), ("z", "x", "y"))
META = 3


def nearest(n):
    return sorted(range(1, n), key=lambda r: min(r, n - r))


def rows_of(value):
    return value.reshape(-1, value.shape[-1])


class Grid:
    def __init__(self, sizes):
        self.n = sizes
        dp, ex = lax.axis_index("dp"), lax.axis_index("expert")
        self.at = {"z": dp // sizes["x"], "x": dp % sizes["x"], "y": ex // 2}
        self.core = ex % 2
        self.sign = 1 - 2 * self.core

    def device(self, axis=None, steps=0):
        at = dict(self.at)
        core = self.core
        if axis is None:
            core = 1 - core
        else:
            n = self.n[axis]
            at[axis] = (at[axis] + self.sign * steps + n) % n
        return (at["z"] * self.n["x"] + at["x"], at["y"] * 2 + core)


def kernel(
    sizes, block_ref, meta_ref, wg_hbm, wu_hbm, wd_hbm, fore_ref, back_ref, place_ref,
    out_ref, dg_ref,
    blocks0, blocks1, blocks2, metas, xt, xc, wg, wu, wd, weights, gate, up, grad,
    hidden, ggrad, ugrad, route0, route1, route2, sib0, sib1, sib2, land0, land1, land2,
    once0, once1, once2, near0, near1, near2, twice0, twice1, twice2, last0, last1, last2,
    load_sem, g1_send, g1_recv, g2_send, g2_recv, g3_send, g3_recv, s_send, s_recv,
    e_send, e_recv, a_send, a_recv, b_send, b_recv, c_send, c_recv,
):
    grid = Grid(sizes)
    nz, nx, ny = sizes["z"], sizes["x"], sizes["y"]
    other = grid.device()

    barrier = pltpu.get_barrier_semaphore()
    around = [other]
    for axis in ("x", "y", "z"):
        around += [grid.device(axis, r) for r in range(1, sizes[axis])]
    for device in around:
        pl.semaphore_signal(barrier, inc=1, device_id=device, device_id_type=MESH)

    loads = [
        pltpu.make_async_copy(src, dst, load_sem.at[i])
        for i, (src, dst) in enumerate(((wg_hbm, wg), (wu_hbm, wu), (wd_hbm, wd)))
    ]
    for load in loads:
        load.start()

    refs = (blocks0, blocks1, blocks2, metas)
    for p in range(PIECES):
        refs[p][0, 0, 0, 0] = block_ref[p]
    metas[0, 0, 0, 0] = meta_ref[...]
    pl.semaphore_wait(barrier, len(around))

    pending = []

    def push(src, dst, ssem, rsem, device):
        copy = pltpu.make_async_remote_copy(
            src_ref=src, dst_ref=dst, send_sem=ssem, recv_sem=rsem,
            device_id=device, device_id_type=MESH,
        )
        copy.start()
        pending.append(copy)

    def arrived(dst, ssem, rsem):
        pltpu.make_async_remote_copy(
            src_ref=dst, dst_ref=dst, send_sem=ssem, recv_sem=rsem,
            device_id=other, device_id_type=MESH,
        ).wait_recv()

    streams = []
    for q, ref in enumerate(refs):
        order = ORDERS[1 if q == META else q]
        streams.append((ref, order, tuple(sizes[a] for a in order)))
    for q, (ref, order, (n1, n2, n3)) in enumerate(streams):
        for r in nearest(n1):
            push(ref.at[0, 0, 0, 0], ref.at[0, 0, 0, n1 - r], g1_send.at[q, r],
                 g1_recv.at[q, n1 - r], grid.device(order[0], r))
    for q, (ref, order, (n1, n2, n3)) in enumerate(streams):
        for r in range(1, n1):
            arrived(ref.at[0, 0, 0, r], g1_send.at[q, r], g1_recv.at[q, r])
        for r in nearest(n2):
            push(ref.at[0, 0, 0], ref.at[0, 0, n2 - r], g2_send.at[q, r],
                 g2_recv.at[q, n2 - r], grid.device(order[1], r))

    def parts_of(q):
        return 1 if q == META else 4

    def turns_of(q):
        return (0,) if q == META else (0, 3, 1, 2)

    have = [{0} for _ in streams]

    def part(ref, lead, q, h):
        n2 = streams[q][2][1]
        size = n2 // parts_of(q)
        return ref.at[lead + (pl.ds(h * size, size),)]

    def share(q, slot):
        ref = refs[q]
        push(ref.at[0, slot], ref.at[1, slot], s_send.at[q, slot], s_recv.at[q, slot], other)

    def shared(q, slot):
        arrived(refs[q].at[1, slot], s_send.at[q, slot], s_recv.at[q, slot])

    def landed(q, way, k, i):
        n3 = streams[q][2][2]
        slot = n3 - k if way == 0 else k
        sem = (q, way, (k - 1) * parts_of(q) + i)
        arrived(part(refs[q], (0, slot), q, turns_of(q)[i]), g3_send.at[sem], g3_recv.at[sem])
        if i == parts_of(q) - 1:
            share(q, slot)

    def hop(q, k, i):
        ref, order, (n1, n2, n3) = streams[q]
        h = turns_of(q)[i]
        if k == 1:
            size = n2 // parts_of(q)
            for r in range(h * size, (h + 1) * size):
                if r not in have[q]:
                    arrived(ref.at[0, 0, r], g2_send.at[q, r], g2_recv.at[q, r])
                    have[q].add(r)
        for way in (0, 1):
            if k > n3 // 2 - way:
                continue
            if k > 1:
                landed(q, way, k - 1, i)
            src = (n3 - (k - 1)) % n3 if way == 0 else k - 1
            dst = n3 - k if way == 0 else k
            sem = (q, way, (k - 1) * parts_of(q) + i)
            push(part(ref, (0, src), q, h), part(ref, (0, dst), q, h), g3_send.at[sem],
                 g3_recv.at[sem], grid.device(order[2], 1 if way == 0 else -1))
        if k == 1 and i == parts_of(q) - 1:
            share(q, 0)

    def spread(p, box, tiles):
        held = box[...]
        tok = held[..., :ROWS, :].reshape(-1, LANES)
        cot = held[..., ROWS:, :].reshape(-1, LANES)
        both = jnp.concatenate([tok, cot], axis=1)
        moved = jnp.dot(fore_ref[p], both, preferred_element_type=F32).astype(BF16)
        for s in range(SEGS):
            columns = slice(p * WIDE + s * LANES, p * WIDE + (s + 1) * LANES)
            for t, tile in enumerate(tiles):
                start = (s * 2 + t) * ROWS
                xt[tile + (slice(None), columns)] = moved[start:start + ROWS, :LANES]
                xc[tile + (slice(None), columns)] = moved[start:start + ROWS, LANES:]

    across = (((1,), (1,)), ((), ()))

    def multiply(p, where):
        columns = slice(p * WIDE, (p + 1) * WIDE)
        tok = rows_of(xt[where + (slice(None), columns)])
        cot = rows_of(xc[where + (slice(None), columns)])
        for acc, lhs, w in ((gate, tok, wg), (up, tok, wu), (grad, cot, wd)):
            add = lax.dot_general(lhs, w[:, columns], across, preferred_element_type=F32)
            old = acc[where]
            acc[where] = old + add.reshape(old.shape)

    everything = slice(None)

    def take0(zi):
        for slot in (2 * zi, 2 * zi + 1):
            shared(0, slot)

        def body(i, _):
            c, yi = i // (ny // 2), i % (ny // 2)
            spread(0, blocks0.at[c, pl.ds(2 * zi, 2), pl.ds(2 * yi, 2)],
                   [(c, zi, yi, 0), (c, zi, yi, 1)])
            return 0

        lax.fori_loop(0, ny, body, 0)
        multiply(0, (everything, zi, everything, everything))

    def take2(yi):
        for slot in (2 * yi, 2 * yi + 1):
            shared(2, slot)

        def body(i, _):
            c, zi = i // (nz // 2), i % (nz // 2)
            spread(2, blocks2.at[c, pl.ds(2 * yi, 2), :, pl.ds(2 * zi, 2)],
                   [(c, zi, yi, 0), (c, zi, yi, 1)])
            return 0

        lax.fori_loop(0, nz, body, 0)
        multiply(2, (everything, everything, yi, everything))

    def take1(xi):
        for slot in (2 * xi, 2 * xi + 1):
            shared(1, slot)
        quads = ny // 4

        def body(i, _):
            c, rest = i // (nz // 2 * quads), i % (nz // 2 * quads)
            zi, yq = rest // quads, rest % quads
            spread(1, blocks1.at[c, pl.ds(2 * xi, 2), pl.ds(2 * zi, 2), pl.ds(4 * yq, 4)],
                   [(c, zi, 2 * yq, xi), (c, zi, 2 * yq + 1, xi)])
            return 0

        lax.fori_loop(0, nz * quads, body, 0)

        def each(c, _):
            multiply(1, (c, everything, everything, xi))
            return 0

        lax.fori_loop(0, 2, each, 0)

    gate[...] = jnp.zeros_like(gate)
    up[...] = jnp.zeros_like(up)
    grad[...] = jnp.zeros_like(grad)

    hops = max(nz, ny) // 2
    items = 4 * hops
    done = {0: set(), 1: set(), 2: set()}

    def complete(q, k):
        n3 = streams[q][2][2]
        return {0} | {n3 - j for j in range(1, k + 1)} | {j for j in range(1, min(k, n3 // 2 - 1) + 1)}

    def ready(q, k):
        n3 = streams[q][2][2]
        k = min(k, n3 // 2)
        here = complete(q, k)
        for pair in range(n3 // 2):
            if pair not in done[q] and {2 * pair, 2 * pair + 1} <= here:
                done[q].add(pair)
                (take0, take1, take2)[q](pair)

    def steps_of(q):
        return streams[q][2][2] // 2 * parts_of(q)

    loaded = False
    for tau in range(items):
        for q in range(len(streams)):
            total = steps_of(q)
            stride = items // total
            if tau % stride == 0:
                i = tau // stride
                hop(q, i // parts_of(q) + 1, i % parts_of(q))
        if tau % 4 == 3 and tau + 1 < items:
            if not loaded:
                for load in loads:
                    load.wait()
                loaded = True
            for q in range(PIECES):
                sent = (tau // (items // steps_of(q)) + 1) // parts_of(q)
                ready(q, sent - 1)
    for q in range(len(streams)):
        n3 = streams[q][2][2]
        for i in range(parts_of(q)):
            for way in (0, 1):
                if n3 // 2 - way > 0:
                    landed(q, way, n3 // 2 - way, i)
    for slot in range(streams[META][2][2]):
        shared(META, slot)
    for q in (0, 2, 1):
        ready(q, streams[q][2][2])

    chips = nz * nx * ny
    expert = lax.axis_index("expert")
    lane = lax.broadcasted_iota(jnp.int32, (chips, LANES), 1)
    columns = []
    for c in range(2):
        meta = metas[c].reshape(chips, LANES)
        column = jnp.concatenate([
            jnp.sum(jnp.where(lane == j * 16 + expert, meta, 0.0), axis=1, keepdims=True)
            for j in range(2)
        ], axis=0)
        high = column.astype(BF16).astype(F32)
        middle = (column - high).astype(BF16).astype(F32)
        columns += [high, middle, column - high - middle]
    lane = lax.broadcasted_iota(jnp.int32, (2 * chips, LANES), 1)
    packed = jnp.zeros((2 * chips, LANES), F32)
    for i, column in enumerate(columns):
        packed = jnp.where(lane == i, column, packed)
    placed = jnp.dot(place_ref[...], packed.astype(BF16), preferred_element_type=F32)
    for c in range(2):
        total = placed[:, 3 * c:3 * c + 1] + placed[:, 3 * c + 1:3 * c + 2]
        total = total + placed[:, 3 * c + 2:3 * c + 3]
        weights[c] = jnp.broadcast_to(total, (2 * chips, LANES)).reshape(weights.shape[1:])

    span = 2 if nz >= 4 else 1
    chunks = nz // 2 // span

    def activate(i, _):
        where = (i // chunks, pl.ds(i % chunks * span, span))
        gate_pre, up_pre, down = rows_of(gate[where]), rows_of(up[where]), rows_of(grad[where])
        weight = rows_of(weights[where])[:, 0:1]
        down = down * weight
        sigma = jax.nn.sigmoid(gate_pre)
        active = gate_pre * sigma
        slope = sigma * (1.0 + gate_pre * (1.0 - sigma))
        shape = hidden[where].shape
        hidden[where] = (active * up_pre * weight).astype(BF16).reshape(shape)
        ggrad[where] = (down * up_pre * slope).astype(BF16).reshape(shape)
        ugrad[where] = (down * active).astype(BF16).reshape(shape)
        return 0

    lax.fori_loop(0, 2 * chunks, activate, 0)

    routes, sibs = (route0, route1, route2), (sib0, sib1, sib2)

    def expand(p, c):
        cols = slice(p * WIDE, (p + 1) * WIDE)

        def body(i, _):
            where = (c, pl.ds(i * span, span))
            term = jnp.dot(rows_of(ggrad[where]), wg[:, cols], preferred_element_type=F32)
            term = term + jnp.dot(rows_of(ugrad[where]), wu[:, cols], preferred_element_type=F32)
            term = term.astype(BF16)
            tile = lambda zi, yi, xi: ((zi * (ny // 2) + yi) * 2 + xi) * ROWS
            groups = []
            for zi in range(span):
                if p == 1:
                    for yq in range(ny // 4):
                        for xi in range(2):
                            starts = [tile(zi, 2 * yq, xi), tile(zi, 2 * yq + 1, xi)]
                            groups.append((zi, yq, xi, starts))
                else:
                    for yi in range(ny // 2):
                        starts = [tile(zi, yi, 0), tile(zi, yi, 1)]
                        groups.append((zi, yi, None, starts))
            for g in range(0, len(groups), 2):
                stacks = []
                for zi, b, xi, starts in groups[g:g + 2]:
                    stacks.append(jnp.concatenate([
                        term[start:start + ROWS, s * LANES:(s + 1) * LANES]
                        for s in range(SEGS) for start in starts
                    ], axis=0))
                moved = jnp.dot(
                    back_ref[p], jnp.concatenate(stacks, axis=1), preferred_element_type=F32
                ).astype(BF16)
                for n, (zi, b, xi, starts) in enumerate(groups[g:g + 2]):
                    value = moved[:, n * LANES:(n + 1) * LANES]
                    z = 2 * (i * span + zi)
                    if p == 0:
                        spot = (c, pl.ds(z, 2), slice(2 * b, 2 * b + 2))
                        value = value.reshape(2, 2, nx, ROWS, LANES)
                    elif p == 1:
                        spot = (c, slice(2 * xi, 2 * xi + 2), pl.ds(z, 2), slice(4 * b, 4 * b + 4))
                        value = value.reshape(2, 2, 4, ROWS, LANES)
                    else:
                        spot = (c, slice(2 * b, 2 * b + 2), slice(None), pl.ds(z, 2))
                        value = value.reshape(2, nx, 2, ROWS, LANES)
                    routes[p][spot] = value
            return 0

        lax.fori_loop(0, chunks, body, 0)

    for p in range(PIECES):
        expand(p, 1)
        push(routes[p].at[1], sibs[p], e_send.at[p], e_recv.at[p], other)
        expand(p, 0)

    lands, onces, nears = (land0, land1, land2), (once0, once1, once2), (near0, near1, near2)
    twices, lasts = (twice0, twice1, twice2), (last0, last1, last2)

    def total(dst, terms, count):
        def body(i, _):
            value = terms[0][i].astype(F32)
            for term in terms[1:]:
                value = value + term[i].astype(F32)
            dst[i] = value.astype(BF16)
            return 0

        lax.fori_loop(0, count, body, 0)

    def reduce_hop(p, t, h):
        order = ORDERS[p]
        n3, n2 = sizes[order[2]], sizes[order[1]]
        size = n2 // 4
        rows = pl.ds(h * size, size)
        for way in (0, 1):
            reach = n3 // 2 - way
            if t > reach:
                continue
            d = reach + 1 - t
            slot = n3 - d if way == 0 else d
            mine, theirs = routes[p].at[0, slot, rows], sibs[p].at[slot, rows]
            sem = (p, way, (t - 1) * 4 + h)
            if t == 1:
                total(theirs, [mine, theirs], size)
                src = theirs
            else:
                src = lands[p].at[way, t - 2, rows]
                before = (p, way, (t - 2) * 4 + h)
                arrived(src, a_send.at[before], a_recv.at[before])
                total(src, [src, mine, theirs], size)
            push(src, lands[p].at[way, t - 1, rows], a_send.at[sem], a_recv.at[sem],
                 grid.device(order[2], -1 if way == 0 else 1))

    chunk = 512

    def descend(i, _):
        cols = pl.ds(pl.multiple_of(i * chunk, chunk), chunk)
        lhs = hidden[...].reshape(4 * chips, hidden.shape[-1])
        rhs = xc[:, :, :, :, :, cols].reshape(4 * chips, chunk)
        dg_ref[:, cols] = lax.dot_general(
            lhs, rhs, (((0,), (0,)), ((), ())), preferred_element_type=F32
        ).astype(BF16)
        return 0

    for p in range(PIECES):
        arrived(sibs[p], e_send.at[p], e_recv.at[p])
    for tau in range(items):
        for p in range(PIECES):
            stride = items // (streams[p][2][2] // 2 * 4)
            if tau % stride == 0:
                i = tau // stride
                reduce_hop(p, i // 4 + 1, i % 4)
        if tau == 3:
            lax.fori_loop(0, 3, descend, 0)
        if tau == 7:
            lax.fori_loop(3, xc.shape[-1] // chunk, descend, 0)

    for p in range(PIECES):
        order = ORDERS[p]
        n1, n2, n3 = streams[p][2]
        terms = [routes[p].at[0, 0], sibs[p].at[0]]
        for way in (0, 1):
            reach = n3 // 2 - way
            if reach > 0:
                for h in range(4):
                    rows = pl.ds(h * (n2 // 4), n2 // 4)
                    sem = (p, way, (reach - 1) * 4 + h)
                    arrived(lands[p].at[way, reach - 1, rows], a_send.at[sem], a_recv.at[sem])
                terms.append(lands[p].at[way, reach - 1])
        total(onces[p], terms, n2)
        for r in nearest(n2):
            push(onces[p].at[r], nears[p].at[r - 1], b_send.at[p, r], b_recv.at[p, r],
                 grid.device(order[1], r))
    for p in range(PIECES):
        order = ORDERS[p]
        n1, n2, n3 = streams[p][2]
        value = onces[p][0].astype(F32)
        for r in nearest(n2):
            arrived(nears[p].at[r - 1], b_send.at[p, r], b_recv.at[p, r])
            value = value + nears[p][r - 1].astype(F32)
        twices[p][...] = value.astype(BF16)
        for r in nearest(n1):
            push(twices[p].at[r], lasts[p].at[r - 1], c_send.at[p, r], c_recv.at[p, r],
                 grid.device(order[0], r))
    for p in range(PIECES):
        n1 = streams[p][2][0]
        value = twices[p][0].astype(F32)
        for r in nearest(n1):
            arrived(lasts[p].at[r - 1], c_send.at[p, r], c_recv.at[p, r])
            value = value + lasts[p][r - 1].astype(F32)
        out_ref[p] = value.astype(BF16)

    for copy in pending:
        copy.wait_send()


def orders_of_rows(sizes):
    result = []
    for p, dims in enumerate((("z", "y", "x"), ("x", "z", "y"), ("y", "x", "z"))):
        long = "y" if p == 1 else "x"
        extent = {a: 4 if a == long else 2 for a in "xyz"}
        rows = []
        for s in range(SEGS):
            for tile in range(2):
                for j in range(2):
                    for z in range(2):
                        for y in range(2):
                            for x in range(2):
                                at = {"z": z, "y": y, "x": x}
                                at[long] += 2 * tile
                                device = 0
                                for a in dims:
                                    device = device * extent[a] + at[a]
                                rows.append((device * 2 + j) * SEGS + s)
        result.append(np.array(rows))
    return result


def order_of_weights(sizes):
    nz, nx, ny = sizes["z"], sizes["x"], sizes["y"]
    source = np.arange(2 * nx * nz * ny).reshape(2, nx // 2, 2, nz // 2, 2, ny // 2, 2)
    return source.transpose(3, 5, 1, 0, 4, 6, 2).reshape(-1)


def build(mesh, sizes):
    nz, nx, ny = sizes["z"], sizes["x"], sizes["y"]
    chips = nz * nx * ny
    experts = 16

    def on_device(tokens, cotangent, route_ids, gate_probs, w_gate, w_up, w_down):
        count, width = tokens.shape
        hid = w_gate.shape[2]
        matches = route_ids[:, :, None] == jnp.arange(experts, dtype=jnp.int32)[None, None, :]
        weights = jnp.sum(jnp.where(matches, gate_probs[:, :, None], 0.0), axis=1)
        meta = jnp.pad(weights.reshape(1, count * experts), ((0, 0), (0, LANES - count * experts)))

        def as_block(v):
            return v.reshape(count, PIECES, SEGS, LANES).transpose(1, 0, 2, 3).reshape(
                PIECES, ROWS, LANES
            )

        block = jnp.concatenate([as_block(tokens), as_block(cotangent)], axis=1)

        def one_hot(source):
            n = source.shape[0]
            return (jnp.asarray(source, jnp.int32)[:, None] == jnp.arange(n)[None, :]).astype(BF16)

        fores = [one_hot(rows) for rows in orders_of_rows(sizes)]
        fore = jnp.stack(fores)
        back = jnp.stack([f.T for f in fores])
        place = one_hot(order_of_weights(sizes))

        n = [tuple(sizes[a] for a in order) for order in ORDERS]
        vm = pl.BlockSpec(memory_space=pltpu.VMEM)
        hbm = pl.BlockSpec(memory_space=pl.ANY)
        dma = pltpu.SemaphoreType.DMA
        tiles = (2, nz // 2, ny // 2, nx // 2, ROWS)
        block_shape = (ROWS, LANES)
        most = max(nz, ny, nx)
        out, down = pl.pallas_call(
            functools.partial(kernel, sizes),
            out_shape=(
                jax.ShapeDtypeStruct((PIECES, ROWS, LANES), BF16),
                jax.ShapeDtypeStruct((hid, width), BF16),
            ),
            in_specs=[vm, vm, hbm, hbm, hbm, vm, vm, vm],
            out_specs=(vm, vm),
            scratch_shapes=[
                *[pltpu.VMEM((2, n3, n2, n1, 2 * ROWS, LANES), BF16) for n1, n2, n3 in n],
                pltpu.VMEM((2, n[1][2], n[1][1], n[1][0], 1, LANES), F32),
                pltpu.VMEM((*tiles, width), BF16),
                pltpu.VMEM((*tiles, width), BF16),
                pltpu.VMEM((hid, width), BF16),
                pltpu.VMEM((hid, width), BF16),
                pltpu.VMEM((hid, width), BF16),
                pltpu.VMEM((*tiles, LANES), F32),
                *[pltpu.VMEM((*tiles, hid), F32) for _ in range(3)],
                *[pltpu.VMEM((*tiles, hid), BF16) for _ in range(3)],
                *[pltpu.VMEM((2, n3, n2, n1, *block_shape), BF16) for n1, n2, n3 in n],
                *[pltpu.VMEM((n3, n2, n1, *block_shape), BF16) for n1, n2, n3 in n],
                *[pltpu.VMEM((2, n3 // 2, n2, n1, *block_shape), BF16) for n1, n2, n3 in n],
                *[pltpu.VMEM((n2, n1, *block_shape), BF16) for n1, n2, n3 in n],
                *[pltpu.VMEM((n2 - 1, n1, *block_shape), BF16) for n1, n2, n3 in n],
                *[pltpu.VMEM((n1, *block_shape), BF16) for n1, n2, n3 in n],
                *[pltpu.VMEM((n1 - 1, *block_shape), BF16) for n1, n2, n3 in n],
                dma((3,)),
                dma((4, most)), dma((4, most)),
                dma((4, most)), dma((4, most)),
                dma((4, 2, 2 * most)), dma((4, 2, 2 * most)),
                dma((4, most)), dma((4, most)),
                dma((3,)), dma((3,)),
                dma((3, 2, 2 * most)), dma((3, 2, 2 * most)),
                dma((3, most)), dma((3, most)),
                dma((3, most)), dma((3, most)),
            ],
            compiler_params=pltpu.CompilerParams(
                collective_id=0, has_side_effects=True, vmem_limit_bytes=62 * 1024 * 1024
            ),
            name="expert_backward",
        )(block, meta, w_gate[0].T, w_up[0].T, w_down[0], fore, back, place)
        grads = out.reshape(PIECES, count, SEGS, LANES).transpose(1, 0, 2, 3).reshape(count, width)
        return grads, down[None]

    both = P(("dp", "expert"), None)
    return jax.shard_map(
        on_device,
        mesh=mesh,
        in_specs=(both, both, both, both, P("expert", None, "dp"), P("expert", None, "dp"),
                  P("expert", "dp", None)),
        out_specs=(both, P("expert", "dp", None)),
        check_vma=False,
    )


def solution(mesh):
    across = 4
    sizes = {"z": mesh.shape["dp"] // across, "x": across, "y": mesh.shape["expert"] // 2}
    return build(mesh, sizes)
```

time: 468 us -> 140 us (0.30)
  waiting for transfers between devices: 394 us -> 0 us
  Pallas kernels: 0 us -> 127 us
  matrix products: 18 us -> 0 us
  starting transfers between devices: 17.7 us -> 0 us
  between operations: 13.8 us -> 0.68 us
  blocking collectives: 13 us -> 0 us
    reduce_scatter x1 -> x0, waiting for transfers between devices: 222 us -> none  [on_device(): lax.psum_scatter((term + lax.dot_general(pair_rows[:, hidden_local:], up_...]
    all_gather x2 -> x0, waiting for transfers between devices: 151 us -> none  [the longest x1 81 us: on_device(): lax.all_gather(rows_grad, 'dp', axis=0, tiled=True)]
    pallas_call x0 -> x1, Pallas kernels: none -> 127 us  [on_device(): pl.pallas_call(functools.partial(kernel, sizes), out_shape=(jax.ShapeDtyp...]
    all_to_all x3 -> x0, waiting for transfers between devices: 20.4 us -> none  [the longest x1 8.21 us: on_device(): lax.all_to_all(send_tokens, 'expert', split_axis=0, concat_axis=0, tiled=...]
    dot_general x9 -> x0, matrix products: 18 us -> none  [the longest x1 3.59 us: backward_rows(): lax.dot_general(hidden, grad_piece, (((0,), (0,)), ((), ())), preferred_e...]
    all_to_all x3 -> x0, starting transfers between devices: 17.6 us -> none  [the longest x1 7.21 us: on_device(): lax.all_to_all(occupied, 'expert', split_axis=0, concat_axis=0, tiled=True)]
    all_to_all x1 -> x0, blocking collectives: 13 us -> none  [on_device(): lax.all_to_all(send_grads, 'expert', split_axis=0, concat_axis=0, tiled=T...]
    unnamed x6 -> x13, local copies, waits for them, and re-layouts: 0.02 us -> 5.69 us
  transfers between devices with their start and end apart: 6 -> 0, of which waited for: 6 -> 0; matrix products, arithmetic and copies ran while one was open for 3% -> 0% of each run, Pallas kernels for 0% -> 0%
where the time goes in v1:
time: 140 us; the launch traced here: 138 us
  Pallas kernels  127 us (91%)
  local copies, waits for them, and re-layouts  7 us (5%)
  other arithmetic  3.73 us (3%)
    pallas_call x1, Pallas kernels, on_device(): pl.pallas_call(functools.partial(kernel, sizes), out_shape=(jax.ShapeDtyp...  127 us
    unnamed x13, local copies, waits for them, and re-layouts  5.69 us

profile of v1, /device:TPU:6, one launch (start us, length us, event | category | flops | bytes accessed | tf_op | source)
XLA Modules:
  0.0 138.0 jit_solution(6669499373727191731)
XLA Ops:
  0.6 0.0 copy-start
  0.6 0.8 select_reduce_fusion
  1.4 0.1 reshape.221
  1.5 0.5 pad.4.meta_ref
  2.0 0.0 copy-done
  2.0 0.7 copy_bitcast_fusion.4
  2.7 0.0 copy-start.3
  2.7 0.6 pad_maximum_fusion.block_ref
  3.3 0.1 copy-done.3
  3.4 0.1 iota_compare_fusion.3
  3.5 0.0 copy-start.2
  3.6 0.7 copy-done.2
  4.2 0.1 iota_compare_fusion.2
  4.3 0.0 copy-start.1
  4.4 0.7 copy-done.1
  5.0 0.1 iota_compare_fusion.1
  5.1 1.1 add_convert_fusion
  6.2 0.0 copy-start.4
  6.2 0.7 copy-done.4
  6.9 0.9 fusion.place_ref
  7.8 126.5 %expert_backward.1 = (bf16[3,16,128]{2,1,0:T(8,128)(2,1)}, bf16[168,3072]{1,0:T(8,128)(2,1)}) custom-call(bf16[3,32,128]{2,1,0:T(8,128)(2,1)} %pad_maximum_fusion.block_ref, f32[1,128]{1,0:T(1,128)} %pad.4.meta_ref, bf16[168,3072]{1,0:T(8,128)(2,1)} %bitcast.37, bf16[168,3072]{1,0:T(8,128)(2,1)} %bitcast.38, bf16[168,3072]{1,0:T(8,128)(2,1)} %bitcast.39, ...), custom_call_target="tpu_custom_call" | custom-call | tf_op jit(solution)/shard_map/expert_backward/pallas_call | solution.py:546
  134.4 0.7 copy_bitcast_fusion.3
  135.1 0.6 copy.30
  135.7 2.2 %copy.32 = bf16[1,168,3072]{2,1,0:T(8,128)(2,1)} copy(bf16[1,168,3072]{2,1,0:T(8,128)(2,1)} %bitcast.40) | data formatting | bytes 2064384
Async XLA Ops:
  0.6 1.4 %copy-start = (bf16[2,3072]{1,0:T(2,128)(2,1)S(1)}, bf16[2,3072]{1,0:T(2,128)(2,1)}, u32[]{:S(2)}) copy-start(bf16[2,3072]{1,0:T(2,128)(2,1)} %param.11) | copy-start | bytes 36868
  2.7 0.7 copy-start.3
  3.5 0.7 copy-start.2
  4.3 0.7 copy-start.1
  6.2 0.7 copy-start.4

commit v2 on v0

v2 whole, which is shorter than its diff:
```python
import functools

import jax
import jax.numpy as jnp
from jax import lax
from jax.experimental import pallas as pl
from jax.experimental.pallas import tpu as pltpu
from jax.sharding import PartitionSpec as P

MESH = pl.DeviceIdType.MESH
F32 = jnp.float32
BF16 = jnp.bfloat16
PIECES = 3
ROWS = 16
LANES = 128
SEGS = 8
WIDE = SEGS * LANES
ORDERS = (("y", "x", "z"), ("y", "z", "x"), ("z", "x", "y"), ("y", "x", "z"))
META = 3


def nearest(n):
    return sorted(range(1, n), key=lambda r: min(r, n - r))


def flat(value):
    return value.reshape(-1, value.shape[-1])


class Grid:
    def __init__(self, sizes):
        self.n = sizes
        dp, ex = lax.axis_index("dp"), lax.axis_index("expert")
        self.at = {"z": dp // sizes["x"], "x": dp % sizes["x"], "y": ex // 2}
        self.core = ex % 2
        self.sign = 1 - 2 * self.core

    def device(self, axis=None, steps=0):
        at = dict(self.at)
        core = self.core
        if axis is None:
            core = 1 - core
        else:
            n = self.n[axis]
            at[axis] = (at[axis] + self.sign * steps + n) % n
        return (at["z"] * self.n["x"] + at["x"], at["y"] * 2 + core)


def one_hot(n, source):
    out = lax.broadcasted_iota(jnp.int32, (n, n), 0)
    return (lax.broadcasted_iota(jnp.int32, (n, n), 1) == source(out)).astype(F32).astype(BF16)


def kernel(
    sizes, tok_ref, cot_ref, ids_ref, probs_ref, wg_hbm, wu_hbm, wd_hbm, out_ref, dg_ref, *scratch
):
    scratch = list(scratch)

    def take(count):
        taken = tuple(scratch[:count])
        del scratch[:count]
        return taken

    first, tiles = take(3), take(3)
    (metas,) = take(1)
    wg, wu, wd, weights = take(4)
    gate, up, grad = take(3), take(3), take(3)
    hidden, ggrad, ugrad = take(3), take(3), take(3)
    routes, sibs, lands, onces, nears = take(3), take(3), take(3), take(3), take(3)
    twices, lasts = take(3), take(3)
    load_sem, g1_send, g1_recv, g2_send, g2_recv, g3_send, g3_recv = take(7)
    s_send, s_recv, e_send, e_recv, a_send, a_recv, b_send, b_recv, c_send, c_recv = take(10)

    grid = Grid(sizes)
    nz, nx, ny = sizes["z"], sizes["x"], sizes["y"]
    n1 = ny
    chips = nz * nx * ny
    other = grid.device()
    dims = [tuple(sizes[a] for a in order) for order in ORDERS]

    barrier = pltpu.get_barrier_semaphore()
    around = [other]
    for axis in ("x", "y", "z"):
        around += [grid.device(axis, r) for r in range(1, sizes[axis])]
    for device in around:
        pl.semaphore_signal(barrier, inc=1, device_id=device, device_id_type=MESH)

    loads = [
        pltpu.make_async_copy(src, dst, load_sem.at[i])
        for i, (src, dst) in enumerate(((wg_hbm, wg), (wu_hbm, wu), (wd_hbm, wd)))
    ]
    for load in loads:
        load.start()

    for half, ref in enumerate((tok_ref, cot_ref)):
        value = ref[...].astype(F32)
        for p in range(PIECES):
            rows = [
                value[:, p * WIDE + s * LANES:p * WIDE + (s + 1) * LANES] for s in range(SEGS)
            ]
            first[p][0, half * ROWS:(half + 1) * ROWS] = jnp.concatenate(rows, axis=0).astype(BF16)
    lane = lax.broadcasted_iota(jnp.int32, (1, LANES), 1)
    meta = jnp.zeros((1, LANES), F32)
    for j in range(ids_ref.shape[0]):
        for k in range(ids_ref.shape[1]):
            meta = meta + jnp.where(
                lane == ids_ref[j:j + 1, k:k + 1] + 16 * j, probs_ref[j:j + 1, k:k + 1], 0.0
            )
    metas[0, 0, 0, 0] = meta
    shift = n1.bit_length() - 1
    fore = one_hot(n1 * ROWS, lambda o: (o & (n1 - 1)) * ROWS + (o >> shift))
    back = one_hot(
        n1 * ROWS, lambda o: (o & (ROWS - 1)) * n1 + (o >> 4)
    )
    swap = one_hot(
        2 * n1 * n1,
        lambda o: (o & (n1 - 1)) * 2 * n1 + ((o >> shift) & 1) * n1 + (o >> (shift + 1)),
    )
    pl.semaphore_wait(barrier, len(around))

    pending = []

    def push(src, dst, ssem, rsem, device):
        copy = pltpu.make_async_remote_copy(
            src_ref=src, dst_ref=dst, send_sem=ssem, recv_sem=rsem,
            device_id=device, device_id_type=MESH,
        )
        copy.start()
        pending.append(copy)

    def arrived(dst, ssem, rsem):
        pltpu.make_async_remote_copy(
            src_ref=dst, dst_ref=dst, send_sem=ssem, recv_sem=rsem,
            device_id=other, device_id_type=MESH,
        ).wait_recv()

    held = [f for f in first] + [metas.at[0, 0, 0]]
    for q in range(4):
        for r in nearest(n1):
            push(held[q].at[0], held[q].at[n1 - r], g1_send.at[q, r], g1_recv.at[q, n1 - r],
                 grid.device(ORDERS[q][0], r))

    grids = list(tiles) + [metas]

    def send2(q, src, r):
        n2 = dims[q][1]
        dst = (src - r) % n2
        push(grids[q].at[0, 0, src], grids[q].at[0, 0, dst], g2_send.at[q, dst],
             g2_recv.at[q, dst], grid.device(ORDERS[q][1], r))

    def got2(q, r):
        arrived(grids[q].at[0, 0, r], g2_send.at[q, r], g2_recv.at[q, r])

    def one_step(q):
        return dims[q][1] <= 4

    for q in (1, 0, 2, META):
        for r in range(1, n1):
            arrived(held[q].at[r], g1_send.at[q, r], g1_recv.at[q, r])
        if q != META:
            both = jnp.concatenate([
                first[q][:, half * ROWS:(half + 1) * ROWS].reshape(n1 * ROWS, LANES)
                for half in range(2)
            ], axis=1)
            moved = jnp.dot(fore, both, preferred_element_type=F32).astype(BF16)
            for s in range(SEGS):
                cols = slice(s * LANES, (s + 1) * LANES)
                for half in range(2):
                    tiles[q][0, 0, 0, half, :, cols] = moved[
                        s * 2 * n1:(s + 1) * 2 * n1, half * LANES:(half + 1) * LANES
                    ]
        n2 = dims[q][1]
        for r in nearest(n2):
            if one_step(q) or min(r, n2 - r) <= 2:
                send2(q, 0, r)

    def turns_of(q):
        return (0,) if q == META else (0, *nearest(dims[q][1]))

    have = [{0} for _ in range(4)]

    def part(q, lead, h):
        return grids[q].at[lead] if q == META else grids[q].at[lead + (h,)]

    def share(q, slot):
        ref = grids[q]
        push(ref.at[0, slot], ref.at[1, slot], s_send.at[q, slot], s_recv.at[q, slot], other)

    def shared(q, slot):
        arrived(grids[q].at[1, slot], s_send.at[q, slot], s_recv.at[q, slot])

    def landed(q, way, k, i):
        n3 = dims[q][2]
        turns = turns_of(q)
        slot = n3 - k if way == 0 else k
        sem = (q, way, (k - 1) * len(turns) + i)
        arrived(part(q, (0, slot), turns[i]), g3_send.at[sem], g3_recv.at[sem])
        if i == len(turns) - 1:
            share(q, slot)

    def second(q, r):
        if r in have[q]:
            return
        n2 = dims[q][1]
        got2(q, r)
        have[q].add(r)
        if not one_step(q):
            if r == 2:
                send2(q, 2, -1)
                send2(q, 2, -2)
            if r == n2 - 2:
                send2(q, n2 - 2, 1)

    def hop(q, k, i):
        n2, n3 = dims[q][1:]
        turns = turns_of(q)
        h = turns[i]
        if k == 1:
            for r in range(n2) if q == META else (h,):
                second(q, r)
        for way in (0, 1):
            reach = n3 // 2 - way
            if 1 < k <= reach + 1:
                landed(q, way, k - 1, i)
            if k > reach:
                continue
            src = (n3 - (k - 1)) % n3 if way == 0 else k - 1
            dst = n3 - k if way == 0 else k
            sem = (q, way, (k - 1) * len(turns) + i)
            push(part(q, (0, src), h), part(q, (0, dst), h), g3_send.at[sem], g3_recv.at[sem],
                 grid.device(ORDERS[q][2], 1 if way == 0 else -1))
        if k == 1 and i == len(turns) - 1:
            share(q, 0)

    across = (((1,), (1,)), ((), ()))

    def multiply(p, at):
        cols = slice(p * WIDE, (p + 1) * WIDE)
        tok = flat(tiles[p][at + (slice(None), 0)])
        cot = flat(tiles[p][at + (slice(None), 1)])
        for acc, lhs, w in ((gate, tok, wg), (up, tok, wu), (grad, cot, wd)):
            result = lax.dot_general(lhs, w[:, cols], across, preferred_element_type=F32)
            acc[p][at] = result.reshape(acc[p].at[at].shape)

    done = set()

    def use(q, slot):
        done.add((q, slot))
        if q == 1:
            shared(1, slot)
            multiply(1, (slice(None), slice(slot, slot + 1)))
        elif (q, slot ^ 1) in done:
            low = slot & ~1
            shared(q, low)
            shared(q, low + 1)
            multiply(q, (slice(None), slice(low, low + 2)))

    hops = nz // 2
    items = 4 * hops
    for tau in range(items):
        for q in (1, 0, 2, META):
            turns = turns_of(q)
            total_items = dims[q][2] // 2 * len(turns)
            stride = items // total_items
            if tau % stride == 0:
                i = tau // stride
                hop(q, i // len(turns) + 1, i % len(turns))
        if tau == 3:
            for load in loads:
                load.wait()
        if tau % 4 == 3:
            k = tau // 4
            for q in (0, 2):
                use(q, (dims[q][2] - k) % dims[q][2])
                if 0 < k <= dims[q][2] // 2 - 1:
                    use(q, k)
            if tau == items // 2 - 1:
                use(1, 0)

    def weigh():
        for slot in range(nz):
            shared(META, slot)
        expert = lax.axis_index("expert")
        lane = lax.broadcasted_iota(jnp.int32, (chips, LANES), 1)
        for c in range(2):
            meta = metas[c].reshape(chips, LANES)
            halves = [
                jnp.broadcast_to(
                    jnp.sum(jnp.where(lane == j * 16 + expert, meta, 0.0), axis=1, keepdims=True),
                    (chips, LANES),
                )
                for j in range(2)
            ]
            for j in range(2):
                weights[c, :, :, j] = halves[j].reshape(nz, nx, ny, LANES)

    for slot in range(1, nx):
        if slot != nx // 2:
            use(1, slot)
    landed(META, 0, nz // 2, 0)
    for q in (0, 2):
        for i in range(len(turns_of(q))):
            landed(q, 0, dims[q][2] // 2, i)
    weigh()
    for q in (0, 2):
        use(q, dims[q][2] // 2)
    for i in range(nz):
        landed(1, 0, nx // 2, i)
    use(1, nx // 2)

    def activate(i, _):
        c, x = i // nx, i % nx
        late = []
        for acc in (gate, up, grad):
            value = flat(acc[2][c, :, x])
            high = value.astype(BF16)
            late += [high, (value - high.astype(F32)).astype(BF16)]
        turned = [jnp.dot(swap, v, preferred_element_type=F32) for v in late]
        gate_pre, up_pre, down = [
            flat(acc[0][c, :, x]) + flat(acc[1][c, x]) + turned[2 * n] + turned[2 * n + 1]
            for n, acc in enumerate((gate, up, grad))
        ]
        weight = flat(weights[c, :, x])[:, 0:1]
        down = down * weight
        sigma = jax.nn.sigmoid(gate_pre)
        active = gate_pre * sigma
        slope = sigma * (1.0 + gate_pre * (1.0 - sigma))
        for ref, value in (
            (hidden, active * up_pre * weight), (ggrad, down * up_pre * slope), (ugrad, down * active)
        ):
            value = value.astype(BF16)
            shape = ref[1].shape[2:]
            ref[0][c, :, x] = value.reshape(shape)
            ref[1][c, x] = value.reshape(shape)
            value = jnp.dot(swap, value, preferred_element_type=F32).astype(BF16)
            ref[2][c, :, x] = value.reshape(shape)
        return 0

    lax.fori_loop(0, 2 * nx, activate, 0)

    def expand(p, c, half):
        cols = slice(p * WIDE, (p + 1) * WIDE)
        n3 = dims[p][2]
        rows = (c, slice(half * n3 // 2, (half + 1) * n3 // 2))
        term = jnp.dot(flat(ggrad[p][rows]), wg[:, cols], preferred_element_type=F32)
        term = term + jnp.dot(flat(ugrad[p][rows]), wu[:, cols], preferred_element_type=F32)
        routes[p][rows] = term.astype(BF16).reshape(routes[p].at[rows].shape)

    def total(dst, terms, index):
        value = terms[0][index].astype(F32)
        for term in terms[1:]:
            value = value + term[index].astype(F32)
        dst[index] = value.astype(BF16)

    def reduce_hop(p, t, h):
        n2, n3 = dims[p][1:]
        for way in (0, 1):
            reach = n3 // 2 - way
            if t > reach:
                continue
            d = reach + 1 - t
            slot = n3 - d if way == 0 else d
            mine, theirs = routes[p].at[0, slot], sibs[p].at[slot]
            sem = (p, way, (t - 1) * n2 + h)
            if t == 1:
                total(theirs, [mine, theirs], h)
                src = theirs.at[h]
            else:
                land = lands[p].at[way, t - 2]
                src = land.at[h]
                before = (p, way, (t - 2) * n2 + h)
                arrived(src, a_send.at[before], a_recv.at[before])
                total(land, [land, mine, theirs], h)
            push(src, lands[p].at[way, t - 1, h], a_send.at[sem], a_recv.at[sem],
                 grid.device(ORDERS[p][2], -1 if way == 0 else 1))

    chunk = WIDE // 2

    def descend(p, half):
        cols = slice(p * WIDE + half * chunk, p * WIDE + (half + 1) * chunk)
        rhs = tiles[p][:, :, :, 1, :, half * chunk:(half + 1) * chunk]
        dg_ref[:, cols] = lax.dot_general(
            flat(hidden[p][...]), flat(rhs), (((0,), (0,)), ((), ())), preferred_element_type=F32
        ).astype(BF16)

    order = (0, 2, 1)
    for p in order:
        n3 = dims[p][2]
        for half in (1, 0):
            expand(p, 1, half)
            some = pl.ds(half * n3 // 2, n3 // 2)
            push(routes[p].at[1, some], sibs[p].at[some], e_send.at[p, half], e_recv.at[p, half],
                 other)
    for p in order:
        n3 = dims[p][2]
        for half in (1, 0):
            expand(p, 0, half)
            some = pl.ds(half * n3 // 2, n3 // 2)
            arrived(sibs[p].at[some], e_send.at[p, half], e_recv.at[p, half])
        for h in range(dims[p][1]):
            reduce_hop(p, 1, h)
    for tau in range(4, items):
        for p in order:
            n2, n3 = dims[p][1:]
            stride = items // (n3 // 2 * n2)
            if tau % stride == 0 and tau // stride >= n2:
                i = tau // stride
                reduce_hop(p, i // n2 + 1, i % n2)
        if tau % 4 == 3:
            k = tau // 4 - 1
            if k < 3:
                descend(k, 0)
                descend(k, 1)

    for p in order:
        n2, n3 = dims[p][1:]
        for h in (*nearest(n2), 0):
            terms = [routes[p].at[0, 0], sibs[p].at[0]]
            for way in (0, 1):
                reach = n3 // 2 - way
                if reach > 0:
                    sem = (p, way, (reach - 1) * n2 + h)
                    land = lands[p].at[way, reach - 1]
                    arrived(land.at[h], a_send.at[sem], a_recv.at[sem])
                    terms.append(land)
            total(onces[p], terms, h)
            if h > 0:
                push(onces[p].at[h], nears[p].at[h - 1], b_send.at[p, h], b_recv.at[p, h],
                     grid.device(ORDERS[p][1], h))
    for p in order:
        n2 = dims[p][1]
        value = onces[p][0].astype(F32)
        for r in nearest(n2):
            arrived(nears[p].at[r - 1], b_send.at[p, r], b_recv.at[p, r])
            value = value + nears[p][r - 1].astype(F32)
        value = value.astype(BF16)
        stack = jnp.concatenate(
            [value[:, s * LANES:(s + 1) * LANES] for s in range(SEGS)], axis=0
        )
        moved = jnp.dot(back, stack, preferred_element_type=F32).astype(BF16)
        twices[p][...] = moved.reshape(n1, ROWS, LANES)
        for r in nearest(n1):
            push(twices[p].at[r], lasts[p].at[r - 1], c_send.at[p, r], c_recv.at[p, r],
                 grid.device(ORDERS[p][0], r))
    for p in order:
        value = twices[p][0].astype(F32)
        for r in nearest(n1):
            arrived(lasts[p].at[r - 1], c_send.at[p, r], c_recv.at[p, r])
            value = value + lasts[p][r - 1].astype(F32)
        count = out_ref.shape[0]
        for s in range(SEGS):
            cols = slice(p * WIDE + s * LANES, p * WIDE + (s + 1) * LANES)
            out_ref[:, cols] = value[s * count:(s + 1) * count].astype(BF16)

    for copy in pending:
        copy.wait_send()


def build(mesh, sizes):
    nz, nx, ny = sizes["z"], sizes["x"], sizes["y"]
    assert ny == nz

    def on_device(tokens, cotangent, route_ids, gate_probs, w_gate, w_up, w_down):
        count, width = tokens.shape
        hid = w_gate.shape[2]
        n = [tuple(sizes[a] for a in order) for order in ORDERS]
        vm = pl.BlockSpec(memory_space=pltpu.VMEM)
        hbm = pl.BlockSpec(memory_space=pl.ANY)
        dma = pltpu.SemaphoreType.DMA
        rows = 2 * ny

        def each(shape_of, dtype=BF16):
            return [pltpu.VMEM(shape_of(*n[p]), dtype) for p in range(PIECES)]

        def sums(dtype):
            return each(lambda n1, n2, n3: (2, n3, n2, rows, hid), dtype)

        most = max(nz, ny, nx)
        out, down = pl.pallas_call(
            functools.partial(kernel, sizes),
            out_shape=(
                jax.ShapeDtypeStruct((count, width), BF16),
                jax.ShapeDtypeStruct((hid, width), BF16),
            ),
            in_specs=[vm, vm, vm, vm, hbm, hbm, hbm],
            out_specs=(vm, vm),
            scratch_shapes=[
                *each(lambda n1, n2, n3: (n1, 2 * ROWS, LANES)),
                *each(lambda n1, n2, n3: (2, n3, n2, 2, rows, WIDE)),
                pltpu.VMEM((2, nz, nx, ny, 1, LANES), F32),
                *[pltpu.VMEM((hid, width), BF16) for _ in range(3)],
                pltpu.VMEM((2, nz, nx, 2, ny, LANES), F32),
                *sums(F32), *sums(F32), *sums(F32),
                *sums(BF16), *sums(BF16), *sums(BF16),
                *each(lambda n1, n2, n3: (2, n3, n2, rows, WIDE)),
                *each(lambda n1, n2, n3: (n3, n2, rows, WIDE)),
                *each(lambda n1, n2, n3: (2, n3 // 2, n2, rows, WIDE)),
                *each(lambda n1, n2, n3: (n2, rows, WIDE)),
                *each(lambda n1, n2, n3: (n2 - 1, rows, WIDE)),
                *each(lambda n1, n2, n3: (n1, ROWS, LANES)),
                *each(lambda n1, n2, n3: (n1 - 1, ROWS, LANES)),
                dma((3,)),
                dma((4, most)), dma((4, most)),
                dma((4, most)), dma((4, most)),
                dma((4, 2, 2 * most)), dma((4, 2, 2 * most)),
                dma((4, most)), dma((4, most)),
                dma((3, 2)), dma((3, 2)),
                dma((3, 2, 2 * most)), dma((3, 2, 2 * most)),
                dma((3, most)), dma((3, most)),
                dma((3, most)), dma((3, most)),
            ],
            compiler_params=pltpu.CompilerParams(
                collective_id=0, has_side_effects=True, vmem_limit_bytes=62 * 1024 * 1024
            ),
            name="expert_backward",
        )(tokens, cotangent, route_ids, gate_probs, w_gate[0].T, w_up[0].T, w_down[0])
        return out, down[None]

    both = P(("dp", "expert"), None)
    return jax.shard_map(
        on_device,
        mesh=mesh,
        in_specs=(both, both, both, both, P("expert", None, "dp"), P("expert", None, "dp"),
                  P("expert", "dp", None)),
        out_specs=(both, P("expert", "dp", None)),
        check_vma=False,
    )


def solution(mesh):
    across = 4
    sizes = {"z": mesh.shape["dp"] // across, "x": across, "y": mesh.shape["expert"] // 2}
    return build(mesh, sizes)
```

time: 468 us -> 110 us (0.24)
  waiting for transfers between devices: 394 us -> 0 us
  Pallas kernels: 0 us -> 105 us
  matrix products: 18 us -> 0 us
  starting transfers between devices: 17.7 us -> 0 us
  between operations: 13.8 us -> 0.64 us
  blocking collectives: 13 us -> 0 us
  other arithmetic: 5.11 us -> 0 us
    reduce_scatter x1 -> x0, waiting for transfers between devices: 222 us -> none  [on_device(): lax.psum_scatter((term + lax.dot_general(pair_rows[:, hidden_local:], up_...]
    all_gather x2 -> x0, waiting for transfers between devices: 151 us -> none  [the longest x1 81 us: on_device(): lax.all_gather(rows_grad, 'dp', axis=0, tiled=True)]
    pallas_call x0 -> x1, Pallas kernels: none -> 105 us  [on_device(): pl.pallas_call(functools.partial(kernel, sizes), out_shape=(jax.ShapeDtyp...]
    all_to_all x3 -> x0, waiting for transfers between devices: 20.4 us -> none  [the longest x1 8.21 us: on_device(): lax.all_to_all(send_tokens, 'expert', split_axis=0, concat_axis=0, tiled=...]
    dot_general x9 -> x0, matrix products: 18 us -> none  [the longest x1 3.59 us: backward_rows(): lax.dot_general(hidden, grad_piece, (((0,), (0,)), ((), ())), preferred_e...]
    all_to_all x3 -> x0, starting transfers between devices: 17.6 us -> none  [the longest x1 7.21 us: on_device(): lax.all_to_all(occupied, 'expert', split_axis=0, concat_axis=0, tiled=True)]
    all_to_all x1 -> x0, blocking collectives: 13 us -> none  [on_device(): lax.all_to_all(send_grads, 'expert', split_axis=0, concat_axis=0, tiled=T...]
  transfers between devices with their start and end apart: 6 -> 0, of which waited for: 6 -> 0; matrix products, arithmetic and copies ran while one was open for 3% -> 0% of each run, Pallas kernels for 0% -> 0%
where the time goes in v2:
time: 110 us; the launch traced here: 109 us
  Pallas kernels  105 us (95%)
  local copies, waits for them, and re-layouts  3.56 us (3%)
    pallas_call x1, Pallas kernels, on_device(): pl.pallas_call(functools.partial(kernel, sizes), out_shape=(jax.ShapeDtyp...  105 us
    unnamed x2, local copies, waits for them, and re-layouts  3.56 us

profile of v2, /device:TPU:6, one launch (start us, length us, event | category | flops | bytes accessed | tf_op | source)
XLA Modules:
  0.0 108.8 jit_solution(6854855690710603622)
XLA Ops:
  0.6 104.6 %expert_backward.1 = (bf16[2,3072]{1,0:T(2,128)(2,1)}, bf16[168,3072]{1,0:T(8,128)(2,1)}) custom-call(bf16[2,3072]{1,0:T(2,128)(2,1)} %tok_ref.1, bf16[2,3072]{1,0:T(2,128)(2,1)} %cot_ref.1, s32[2,4]{1,0:T(2,128)} %ids_ref.1, f32[2,4]{1,0:T(2,128)} %probs_ref.1, bf16[168,3072]{1,0:T(8,128)(2,1)} %bitcast.8, bf16[168,3072]{1,0:T(8,128)(2,1)} %bitcast.9, ...), custom_call_target="tpu_custom_call" | custom-call | tf_op jit(solution)/shard_map/expert_backward/pallas_call | solution.py:479
  105.2 1.3 %copy.11 = bf16[2,3072]{1,0:T(2,128)(2,1)} copy(bf16[2,3072]{1,0:T(2,128)(2,1)} %get-tuple-element.8) | data formatting | bytes 24576
  106.5 2.2 %copy.12 = bf16[1,168,3072]{2,1,0:T(8,128)(2,1)} copy(bf16[1,168,3072]{2,1,0:T(8,128)(2,1)} %bitcast.11) | data formatting | bytes 2064384

commit v3 on v2

--- a/solution.py
+++ b/solution.py
@@ -68,8 +68,10 @@
     hidden, ggrad, ugrad = take(3), take(3), take(3)
     routes, sibs, lands, onces, nears = take(3), take(3), take(3), take(3), take(3)
     twices, lasts = take(3), take(3)
-    load_sem, g1_send, g1_recv, g2_send, g2_recv, g3_send, g3_recv = take(7)
-    s_send, s_recv, e_send, e_recv, a_send, a_recv, b_send, b_recv, c_send, c_recv = take(10)
+    (dg,) = take(1)
+    opposite = take(3)
+    load_sem, sent, g1_recv, g2_recv, g3_recv, s_recv = take(6)
+    e_recv, o_recv, a_recv, b_recv, c_recv = take(5)
 
     grid = Grid(sizes)
     nz, nx, ny = sizes["z"], sizes["x"], sizes["y"]
@@ -118,26 +120,25 @@
     )
     pl.semaphore_wait(barrier, len(around))
 
-    pending = []
-
-    def push(src, dst, ssem, rsem, device):
-        copy = pltpu.make_async_remote_copy(
+    def copy_of(src, dst, ssem, rsem, device):
+        return pltpu.make_async_remote_copy(
             src_ref=src, dst_ref=dst, send_sem=ssem, recv_sem=rsem,
             device_id=device, device_id_type=MESH,
         )
-        copy.start()
-        pending.append(copy)
-
-    def arrived(dst, ssem, rsem):
-        pltpu.make_async_remote_copy(
-            src_ref=dst, dst_ref=dst, send_sem=ssem, recv_sem=rsem,
-            device_id=other, device_id_type=MESH,
-        ).wait_recv()
+
+    def push(src, dst, kind, q, rsem, device):
+        copy_of(src, dst, sent.at[kind, q], rsem, device).start()
+
+    def arrived(dst, rsem):
+        copy_of(dst, dst, sent.at[0, 0], rsem, other).wait_recv()
+
+    def drain(ref, kind, q):
+        copy_of(ref, ref, sent.at[kind, q], g1_recv.at[0], other).wait_send()
 
     held = [f for f in first] + [metas.at[0, 0, 0]]
     for q in range(4):
         for r in nearest(n1):
-            push(held[q].at[0], held[q].at[n1 - r], g1_send.at[q, r], g1_recv.at[q, n1 - r],
+            push(held[q].at[0], held[q].at[n1 - r], 0, q, g1_recv.at[q],
                  grid.device(ORDERS[q][0], r))
 
     grids = list(tiles) + [metas]
@@ -145,18 +146,17 @@
     def send2(q, src, r):
         n2 = dims[q][1]
         dst = (src - r) % n2
-        push(grids[q].at[0, 0, src], grids[q].at[0, 0, dst], g2_send.at[q, dst],
-             g2_recv.at[q, dst], grid.device(ORDERS[q][1], r))
+        push(grids[q].at[0, 0, src], grids[q].at[0, 0, dst], 1, q, g2_recv.at[q, dst],
+             grid.device(ORDERS[q][1], r))
 
     def got2(q, r):
-        arrived(grids[q].at[0, 0, r], g2_send.at[q, r], g2_recv.at[q, r])
+        arrived(grids[q].at[0, 0, r], g2_recv.at[q, r])
 
     def one_step(q):
         return dims[q][1] <= 4
 
     for q in (1, 0, 2, META):
-        for r in range(1, n1):
-            arrived(held[q].at[r], g1_send.at[q, r], g1_recv.at[q, r])
+        arrived(held[q].at[pl.ds(1, n1 - 1)], g1_recv.at[q])
         if q != META:
             both = jnp.concatenate([
                 first[q][:, half * ROWS:(half + 1) * ROWS].reshape(n1 * ROWS, LANES)
@@ -175,26 +175,27 @@
                 send2(q, 0, r)
 
     def turns_of(q):
-        return (0,) if q == META else (0, *nearest(dims[q][1]))
+        return {0: (0, 1), 1: (0, 3, 1, 2), 2: (0, 1), META: (0,)}[q]
 
     have = [{0} for _ in range(4)]
 
     def part(q, lead, h):
-        return grids[q].at[lead] if q == META else grids[q].at[lead + (h,)]
+        return grids[q].at[lead] if q == META else grids[q].at[lead + (pl.ds(2 * h, 2),)]
 
     def share(q, slot):
         ref = grids[q]
-        push(ref.at[0, slot], ref.at[1, slot], s_send.at[q, slot], s_recv.at[q, slot], other)
+        if q != META:
+            push(ref.at[0, slot], ref.at[1, slot], 3, q, s_recv.at[q, slot], other)
 
     def shared(q, slot):
-        arrived(grids[q].at[1, slot], s_send.at[q, slot], s_recv.at[q, slot])
+        arrived(grids[q].at[1, slot], s_recv.at[q, slot])
 
     def landed(q, way, k, i):
         n3 = dims[q][2]
         turns = turns_of(q)
         slot = n3 - k if way == 0 else k
         sem = (q, way, (k - 1) * len(turns) + i)
-        arrived(part(q, (0, slot), turns[i]), g3_send.at[sem], g3_recv.at[sem])
+        arrived(part(q, (0, slot), turns[i]), g3_recv.at[sem])
         if i == len(turns) - 1:
             share(q, slot)
 
@@ -216,7 +217,7 @@
         turns = turns_of(q)
         h = turns[i]
         if k == 1:
-            for r in range(n2) if q == META else (h,):
+            for r in range(n2) if q == META else (2 * h, 2 * h + 1):
                 second(q, r)
         for way in (0, 1):
             reach = n3 // 2 - way
@@ -227,7 +228,7 @@
             src = (n3 - (k - 1)) % n3 if way == 0 else k - 1
             dst = n3 - k if way == 0 else k
             sem = (q, way, (k - 1) * len(turns) + i)
-            push(part(q, (0, src), h), part(q, (0, dst), h), g3_send.at[sem], g3_recv.at[sem],
+            push(part(q, (0, src), h), part(q, (0, dst), h), 2, q, g3_recv.at[sem],
                  grid.device(ORDERS[q][2], 1 if way == 0 else -1))
         if k == 1 and i == len(turns) - 1:
             share(q, 0)
@@ -255,31 +256,31 @@
             shared(q, low + 1)
             multiply(q, (slice(None), slice(low, low + 2)))
 
-    hops = nz // 2
-    items = 4 * hops
+    items = 8
+    starts = ((0, 1, 3, 3), (2, 4, 6, 7))
     for tau in range(items):
-        for q in (1, 0, 2, META):
-            turns = turns_of(q)
-            total_items = dims[q][2] // 2 * len(turns)
-            stride = items // total_items
-            if tau % stride == 0:
-                i = tau // stride
-                hop(q, i // len(turns) + 1, i % len(turns))
-        if tau == 3:
+        for q in (0, 2):
+            hop(q, tau // 2 + 1, tau % 2)
+        for k in range(2):
+            for i in range(4):
+                if starts[k][i] == tau:
+                    hop(1, k + 1, i)
+        if tau % 2 == 0:
+            hop(META, tau // 2 + 1, 0)
+        if tau == 1:
             for load in loads:
                 load.wait()
-        if tau % 4 == 3:
-            k = tau // 4
+        if tau % 2 == 1:
+            k = tau // 2
             for q in (0, 2):
                 use(q, (dims[q][2] - k) % dims[q][2])
                 if 0 < k <= dims[q][2] // 2 - 1:
                     use(q, k)
-            if tau == items // 2 - 1:
-                use(1, 0)
+        if tau == 6:
+            use(1, 0)
 
     def weigh():
-        for slot in range(nz):
-            shared(META, slot)
+        arrived(metas.at[1], s_recv.at[META, 0])
         expert = lax.axis_index("expert")
         lane = lax.broadcasted_iota(jnp.int32, (chips, LANES), 1)
         for c in range(2):
@@ -298,13 +299,14 @@
         if slot != nx // 2:
             use(1, slot)
     landed(META, 0, nz // 2, 0)
+    push(metas.at[0], metas.at[1], 3, META, s_recv.at[META, 0], other)
+    weigh()
     for q in (0, 2):
         for i in range(len(turns_of(q))):
             landed(q, 0, dims[q][2] // 2, i)
-    weigh()
     for q in (0, 2):
         use(q, dims[q][2] // 2)
-    for i in range(nz):
+    for i in range(len(turns_of(1))):
         landed(1, 0, nx // 2, i)
     use(1, nx // 2)
 
@@ -346,32 +348,47 @@
         term = term + jnp.dot(flat(ugrad[p][rows]), wu[:, cols], preferred_element_type=F32)
         routes[p][rows] = term.astype(BF16).reshape(routes[p].at[rows].shape)
 
-    def total(dst, terms, index):
-        value = terms[0][index].astype(F32)
-        for term in terms[1:]:
-            value = value + term[index].astype(F32)
-        dst[index] = value.astype(BF16)
+    def total(dst, terms, indices):
+        for index in indices:
+            value = terms[0][index].astype(F32)
+            for term in terms[1:]:
+                value = value + term[index].astype(F32)
+            dst[index] = value.astype(BF16)
+
+    def reach_of(p, way):
+        n3 = dims[p][2]
+        return 3 if n3 == 8 else n3 // 2 - way
 
     def reduce_hop(p, t, h):
         n2, n3 = dims[p][1:]
+        rows, some = (2 * h, 2 * h + 1), pl.ds(2 * h, 2)
+        parts = n2 // 2
+        if t == 1 and n3 == 8:
+            theirs = sibs[p].at[4]
+            total(theirs, [routes[p].at[0, 4], theirs], rows)
+            push(theirs.at[some], opposite[p].at[some], 5, p, o_recv.at[p, h],
+                 grid.device(ORDERS[p][2], -2))
         for way in (0, 1):
-            reach = n3 // 2 - way
+            reach = reach_of(p, way)
             if t > reach:
                 continue
             d = reach + 1 - t
             slot = n3 - d if way == 0 else d
             mine, theirs = routes[p].at[0, slot], sibs[p].at[slot]
-            sem = (p, way, (t - 1) * n2 + h)
+            sem = (p, way, (t - 1) * parts + h)
             if t == 1:
-                total(theirs, [mine, theirs], h)
-                src = theirs.at[h]
+                total(theirs, [mine, theirs], rows)
+                src = theirs.at[some]
             else:
                 land = lands[p].at[way, t - 2]
-                src = land.at[h]
-                before = (p, way, (t - 2) * n2 + h)
-                arrived(src, a_send.at[before], a_recv.at[before])
-                total(land, [land, mine, theirs], h)
-            push(src, lands[p].at[way, t - 1, h], a_send.at[sem], a_recv.at[sem],
+                src = land.at[some]
+                terms = [land, mine, theirs]
+                if n3 == 8 and t == 2 and way == 0:
+                    arrived(opposite[p].at[some], o_recv.at[p, h])
+                    terms.append(opposite[p])
+                arrived(src, a_recv.at[p, way, (t - 2) * parts + h])
+                total(land, terms, rows)
+            push(src, lands[p].at[way, t - 1, some], 5, p, a_recv.at[sem],
                  grid.device(ORDERS[p][2], -1 if way == 0 else 1))
 
     chunk = WIDE // 2
@@ -379,59 +396,73 @@
     def descend(p, half):
         cols = slice(p * WIDE + half * chunk, p * WIDE + (half + 1) * chunk)
         rhs = tiles[p][:, :, :, 1, :, half * chunk:(half + 1) * chunk]
-        dg_ref[:, cols] = lax.dot_general(
+        dg[:, cols] = lax.dot_general(
             flat(hidden[p][...]), flat(rhs), (((0,), (0,)), ((), ())), preferred_element_type=F32
         ).astype(BF16)
 
-    order = (0, 2, 1)
-    for p in order:
+    def hand_over(p):
         n3 = dims[p][2]
         for half in (1, 0):
             expand(p, 1, half)
             some = pl.ds(half * n3 // 2, n3 // 2)
-            push(routes[p].at[1, some], sibs[p].at[some], e_send.at[p, half], e_recv.at[p, half],
-                 other)
-    for p in order:
+            push(routes[p].at[1, some], sibs[p].at[some], 4, p, e_recv.at[p, half], other)
+
+    def set_out(p):
         n3 = dims[p][2]
         for half in (1, 0):
             expand(p, 0, half)
+        for half in (1, 0):
             some = pl.ds(half * n3 // 2, n3 // 2)
-            arrived(sibs[p].at[some], e_send.at[p, half], e_recv.at[p, half])
-        for h in range(dims[p][1]):
+            arrived(sibs[p].at[some], e_recv.at[p, half])
+        for h in range(dims[p][1] // 2):
             reduce_hop(p, 1, h)
-    for tau in range(4, items):
-        for p in order:
-            n2, n3 = dims[p][1:]
-            stride = items // (n3 // 2 * n2)
-            if tau % stride == 0 and tau // stride >= n2:
-                i = tau // stride
-                reduce_hop(p, i // n2 + 1, i % n2)
-        if tau % 4 == 3:
-            k = tau // 4 - 1
-            if k < 3:
-                descend(k, 0)
-                descend(k, 1)
-
-    for p in order:
+
+    def settle(p, h):
         n2, n3 = dims[p][1:]
-        for h in (*nearest(n2), 0):
-            terms = [routes[p].at[0, 0], sibs[p].at[0]]
-            for way in (0, 1):
-                reach = n3 // 2 - way
-                if reach > 0:
-                    sem = (p, way, (reach - 1) * n2 + h)
-                    land = lands[p].at[way, reach - 1]
-                    arrived(land.at[h], a_send.at[sem], a_recv.at[sem])
-                    terms.append(land)
-            total(onces[p], terms, h)
-            if h > 0:
-                push(onces[p].at[h], nears[p].at[h - 1], b_send.at[p, h], b_recv.at[p, h],
-                     grid.device(ORDERS[p][1], h))
+        rows, some = (2 * h, 2 * h + 1), pl.ds(2 * h, 2)
+        terms = [routes[p].at[0, 0], sibs[p].at[0]]
+        for way in (0, 1):
+            reach = reach_of(p, way)
+            land = lands[p].at[way, reach - 1]
+            arrived(land.at[some], a_recv.at[p, way, (reach - 1) * (n2 // 2) + h])
+            terms.append(land)
+        total(onces[p], terms, rows)
+        for r in rows:
+            if r > 0:
+                push(onces[p].at[r], nears[p].at[r - 1], 6, p, b_recv.at[p],
+                     grid.device(ORDERS[p][1], r))
+
+    hand_over(0)
+    hand_over(2)
+    set_out(0)
+    hand_over(1)
+    set_out(2)
+    set_out(1)
+    for tau in range(2, 6):
+        for p in (0, 2):
+            reduce_hop(p, tau // 2 + 1, tau % 2)
+        if tau == 3:
+            for h in (0, 1, 2, 3):
+                reduce_hop(1, 2, h)
+            for p in range(PIECES):
+                descend(p, 0)
+        if tau == 5:
+            for h in (0, 1, 2, 3):
+                settle(1, h)
+    for p in range(PIECES):
+        descend(p, 1)
+    store = pltpu.make_async_copy(dg, dg_ref, load_sem.at[0])
+    store.start()
+    for h in (0, 1):
+        for p in (0, 2):
+            settle(p, h)
+
+    order = (0, 2, 1)
     for p in order:
         n2 = dims[p][1]
         value = onces[p][0].astype(F32)
+        arrived(nears[p], b_recv.at[p])
         for r in nearest(n2):
-            arrived(nears[p].at[r - 1], b_send.at[p, r], b_recv.at[p, r])
             value = value + nears[p][r - 1].astype(F32)
         value = value.astype(BF16)
         stack = jnp.concatenate(
@@ -440,20 +471,31 @@
         moved = jnp.dot(back, stack, preferred_element_type=F32).astype(BF16)
         twices[p][...] = moved.reshape(n1, ROWS, LANES)
         for r in nearest(n1):
-            push(twices[p].at[r], lasts[p].at[r - 1], c_send.at[p, r], c_recv.at[p, r],
+            push(twices[p].at[r], lasts[p].at[r - 1], 7, p, c_recv.at[p],
                  grid.device(ORDERS[p][0], r))
     for p in order:
         value = twices[p][0].astype(F32)
+        arrived(lasts[p], c_recv.at[p])
         for r in nearest(n1):
-            arrived(lasts[p].at[r - 1], c_send.at[p, r], c_recv.at[p, r])
             value = value + lasts[p][r - 1].astype(F32)
         count = out_ref.shape[0]
         for s in range(SEGS):
             cols = slice(p * WIDE + s * LANES, p * WIDE + (s + 1) * LANES)
             out_ref[:, cols] = value[s * count:(s + 1) * count].astype(BF16)
 
-    for copy in pending:
-        copy.wait_send()
+    for q in range(4):
+        n2, n3 = dims[q][1:]
+        drain(held[q].at[pl.ds(0, n1 - 1)], 0, q)
+        drain(grids[q].at[0, 0, pl.ds(0, n2 - 1)], 1, q)
+        drain(grids[q].at[0, pl.ds(0, n3 - 1)], 2, q)
+        drain(grids[q].at[0], 3, q)
+    for p in range(PIECES):
+        n2, n3 = dims[p][1:]
+        drain(routes[p].at[1], 4, p)
+        drain(sibs[p].at[pl.ds(0, n3 - 1)], 5, p)
+        drain(onces[p].at[pl.ds(0, n2 - 1)], 6, p)
+        drain(twices[p].at[pl.ds(0, n1 - 1)], 7, p)
+    store.wait()
 
 
 def build(mesh, sizes):
@@ -483,7 +525,7 @@
                 jax.ShapeDtypeStruct((hid, width), BF16),
             ),
             in_specs=[vm, vm, vm, vm, hbm, hbm, hbm],
-            out_specs=(vm, vm),
+            out_specs=(vm, hbm),
             scratch_shapes=[
                 *each(lambda n1, n2, n3: (n1, 2 * ROWS, LANES)),
                 *each(lambda n1, n2, n3: (2, n3, n2, 2, rows, WIDE)),
@@ -499,15 +541,19 @@
                 *each(lambda n1, n2, n3: (n2 - 1, rows, WIDE)),
                 *each(lambda n1, n2, n3: (n1, ROWS, LANES)),
                 *each(lambda n1, n2, n3: (n1 - 1, ROWS, LANES)),
+                pltpu.VMEM((hid, width), BF16),
+                *each(lambda n1, n2, n3: (n2, rows, WIDE)),
                 dma((3,)),
-                dma((4, most)), dma((4, most)),
-                dma((4, most)), dma((4, most)),
-                dma((4, 2, 2 * most)), dma((4, 2, 2 * most)),
-                dma((4, most)), dma((4, most)),
-                dma((3, 2)), dma((3, 2)),
-                dma((3, 2, 2 * most)), dma((3, 2, 2 * most)),
-                dma((3, most)), dma((3, most)),
-                dma((3, most)), dma((3, most)),
+                dma((8, 4)),
+                dma((4,)),
+                dma((4, most)),
+                dma((4, 2, most)),
+                dma((4, most)),
+                dma((3, 2)),
+                dma((3, 2)),
+                dma((3, 2, most)),
+                dma((3,)),
+                dma((3,)),
             ],
             compiler_params=pltpu.CompilerParams(
                 collective_id=0, has_side_effects=True, vmem_limit_bytes=62 * 1024 * 1024

time: 110 us -> 106 us (0.964)
  Pallas kernels: 105 us -> 99.5 us
    pallas_call x1, Pallas kernels: 105 us -> 99.5 us  [on_device(): pl.pallas_call(functools.partial(kernel, sizes), out_shape=(jax.ShapeDtyp...]
where the time goes in v3:
time: 106 us; the launch traced here: 104 us
  Pallas kernels  99.5 us (94%)
  local copies, waits for them, and re-layouts  3.56 us (3%)
    pallas_call x1, Pallas kernels, on_device(): pl.pallas_call(functools.partial(kernel, sizes), out_shape=(jax.ShapeDtyp...  99.5 us
    unnamed x2, local copies, waits for them, and re-layouts  3.56 us

profile of v3, /device:TPU:6, one launch (start us, length us, event | category | flops | bytes accessed | tf_op | source)
XLA Modules:
  0.0 103.7 jit_solution(12632397626813338598)
XLA Ops:
  0.6 99.5 %expert_backward.1 = (bf16[2,3072]{1,0:T(2,128)(2,1)}, bf16[168,3072]{1,0:T(8,128)(2,1)}) custom-call(bf16[2,3072]{1,0:T(2,128)(2,1)} %tok_ref.1, bf16[2,3072]{1,0:T(2,128)(2,1)} %cot_ref.1, s32[2,4]{1,0:T(2,128)} %ids_ref.1, f32[2,4]{1,0:T(2,128)} %probs_ref.1, bf16[168,3072]{1,0:T(8,128)(2,1)} %bitcast.8, bf16[168,3072]{1,0:T(8,128)(2,1)} %bitcast.9, ...), custom_call_target="tpu_custom_call" | custom-call | tf_op jit(solution)/shard_map/expert_backward/pallas_call | solution.py:521
  100.2 1.3 %copy.11 = bf16[2,3072]{1,0:T(2,128)(2,1)} copy(bf16[2,3072]{1,0:T(2,128)(2,1)} %get-tuple-element.8) | data formatting | bytes 24576
  101.5 2.2 %copy.12 = bf16[1,168,3072]{2,1,0:T(8,128)(2,1)} copy(bf16[1,168,3072]{2,1,0:T(8,128)(2,1)} %bitcast.11) | data formatting | bytes 2064384

commit v4 on v3

--- a/solution.py
+++ b/solution.py
@@ -15,7 +15,7 @@
 LANES = 128
 SEGS = 8
 WIDE = SEGS * LANES
-ORDERS = (("y", "x", "z"), ("y", "z", "x"), ("z", "x", "y"), ("y", "x", "z"))
+ORDERS = (("y", "x", "z"), ("yz", "zy", "x"), ("z", "x", "y"), ("y", "x", "z"))
 META = 3
 
 
@@ -40,6 +40,10 @@
         core = self.core
         if axis is None:
             core = 1 - core
+        elif len(axis) == 2:
+            for name, here in zip(axis, (1 - core, core)):
+                n = self.n[name]
+                at[name] = (at[name] + self.sign * here * steps + n) % n
         else:
             n = self.n[axis]
             at[axis] = (at[axis] + self.sign * steps + n) % n
@@ -70,6 +74,7 @@
     twices, lasts = take(3), take(3)
     (dg,) = take(1)
     opposite = take(3)
+    (turns,) = take(1)
     load_sem, sent, g1_recv, g2_recv, g3_recv, s_recv = take(6)
     e_recv, o_recv, a_recv, b_recv, c_recv = take(5)
 
@@ -78,7 +83,7 @@
     n1 = ny
     chips = nz * nx * ny
     other = grid.device()
-    dims = [tuple(sizes[a] for a in order) for order in ORDERS]
+    dims = [tuple(sizes[a[0]] for a in order) for order in ORDERS]
 
     barrier = pltpu.get_barrier_semaphore()
     around = [other]
@@ -114,10 +119,16 @@
     back = one_hot(
         n1 * ROWS, lambda o: (o & (ROWS - 1)) * n1 + (o >> 4)
     )
+    span = 2 * n1 * n1
     swap = one_hot(
-        2 * n1 * n1,
-        lambda o: (o & (n1 - 1)) * 2 * n1 + ((o >> shift) & 1) * n1 + (o >> (shift + 1)),
-    )
+        span, lambda o: (o & (n1 - 1)) * 2 * n1 + ((o >> shift) & 1) * n1 + (o >> (shift + 1))
+    ).astype(F32)
+    same = one_hot(span, lambda o: o).astype(F32)
+    for c in range(2):
+        on_z = ((grid.core + c) % 2).astype(F32)
+        turn = same * (1.0 - on_z) + swap * on_z
+        turns[c, :, :span] = swap.astype(BF16)
+        turns[c, :, span:] = turn.astype(BF16)
     pl.semaphore_wait(barrier, len(around))
 
     def copy_of(src, dst, ssem, rsem, device):
@@ -257,7 +268,7 @@
             multiply(q, (slice(None), slice(low, low + 2)))
 
     items = 8
-    starts = ((0, 1, 3, 3), (2, 4, 6, 7))
+    starts = ((0, 1, 4, 5), (2, 3, 6, 7))
     for tau in range(items):
         for q in (0, 2):
             hop(q, tau // 2 + 1, tau % 2)
@@ -265,6 +276,8 @@
             for i in range(4):
                 if starts[k][i] == tau:
                     hop(1, k + 1, i)
+        if tau == 1:
+            second(1, 2)
         if tau % 2 == 0:
             hop(META, tau // 2 + 1, 0)
         if tau == 1:
@@ -312,16 +325,17 @@
 
     def activate(i, _):
         c, x = i // nx, i % nx
-        late = []
+        both = turns[c]
+        sums = []
         for acc in (gate, up, grad):
-            value = flat(acc[2][c, :, x])
+            value = jnp.concatenate([flat(acc[2][c, :, x]), flat(acc[1][c, x])], axis=0)
             high = value.astype(BF16)
-            late += [high, (value - high.astype(F32)).astype(BF16)]
-        turned = [jnp.dot(swap, v, preferred_element_type=F32) for v in late]
-        gate_pre, up_pre, down = [
-            flat(acc[0][c, :, x]) + flat(acc[1][c, x]) + turned[2 * n] + turned[2 * n + 1]
-            for n, acc in enumerate((gate, up, grad))
-        ]
+            low = (value - high.astype(F32)).astype(BF16)
+            sums.append(
+                flat(acc[0][c, :, x]) + jnp.dot(both, high, preferred_element_type=F32)
+                + jnp.dot(both, low, preferred_element_type=F32)
+            )
+        gate_pre, up_pre, down = sums
         weight = flat(weights[c, :, x])[:, 0:1]
         down = down * weight
         sigma = jax.nn.sigmoid(gate_pre)
@@ -333,12 +347,14 @@
             value = value.astype(BF16)
             shape = ref[1].shape[2:]
             ref[0][c, :, x] = value.reshape(shape)
-            ref[1][c, x] = value.reshape(shape)
-            value = jnp.dot(swap, value, preferred_element_type=F32).astype(BF16)
-            ref[2][c, :, x] = value.reshape(shape)
+            for p, at in ((1, (c, x)), (2, (c, slice(None), x))):
+                turn = both[:, :span] if p == 2 else both[:, span:]
+                moved = jnp.dot(turn, value, preferred_element_type=F32).astype(BF16)
+                ref[p][at] = moved.reshape(shape)
         return 0
 
-    lax.fori_loop(0, 2 * nx, activate, 0)
+    for i in range(2 * nx):
+        activate(i, 0)
 
     def expand(p, c, half):
         cols = slice(p * WIDE, (p + 1) * WIDE)
@@ -432,23 +448,23 @@
                 push(onces[p].at[r], nears[p].at[r - 1], 6, p, b_recv.at[p],
                      grid.device(ORDERS[p][1], r))
 
+    hand_over(1)
     hand_over(0)
+    set_out(1)
     hand_over(2)
     set_out(0)
-    hand_over(1)
     set_out(2)
-    set_out(1)
     for tau in range(2, 6):
         for p in (0, 2):
             reduce_hop(p, tau // 2 + 1, tau % 2)
         if tau == 3:
-            for h in (0, 1, 2, 3):
-                reduce_hop(1, 2, h)
             for p in range(PIECES):
                 descend(p, 0)
-        if tau == 5:
-            for h in (0, 1, 2, 3):
-                settle(1, h)
+        if tau in (3, 4):
+            for h in (2 * tau - 6, 2 * tau - 5):
+                reduce_hop(1, 2, h)
+    for h in range(4):
+        settle(1, h)
     for p in range(PIECES):
         descend(p, 1)
     store = pltpu.make_async_copy(dg, dg_ref, load_sem.at[0])
@@ -505,7 +521,7 @@
     def on_device(tokens, cotangent, route_ids, gate_probs, w_gate, w_up, w_down):
         count, width = tokens.shape
         hid = w_gate.shape[2]
-        n = [tuple(sizes[a] for a in order) for order in ORDERS]
+        n = [tuple(sizes[a[0]] for a in order) for order in ORDERS]
         vm = pl.BlockSpec(memory_space=pltpu.VMEM)
         hbm = pl.BlockSpec(memory_space=pl.ANY)
         dma = pltpu.SemaphoreType.DMA
@@ -543,6 +559,7 @@
                 *each(lambda n1, n2, n3: (n1 - 1, ROWS, LANES)),
                 pltpu.VMEM((hid, width), BF16),
                 *each(lambda n1, n2, n3: (n2, rows, WIDE)),
+                pltpu.VMEM((2, rows * nz, 2 * rows * nz), BF16),
                 dma((3,)),
                 dma((8, 4)),
                 dma((4,)),

time: 106 us -> 101 us (0.953); the launches traced: 104 us -> 101 us
  Pallas kernels: 99.5 us -> 96.6 us
    pallas_call x1, Pallas kernels: 99.5 us -> 96.6 us  [on_device(): pl.pallas_call(functools.partial(kernel, sizes), out_shape=(jax.ShapeDtyp...]
where the time goes in v4:
time: 101 us
  Pallas kernels  96.6 us (96%)
  local copies, waits for them, and re-layouts  3.56 us (4%)
    pallas_call x1, Pallas kernels, on_device(): pl.pallas_call(functools.partial(kernel, sizes), out_shape=(jax.ShapeDtyp...  96.6 us
    unnamed x2, local copies, waits for them, and re-layouts  3.56 us

profile of v4, /device:TPU:6, one launch (start us, length us, event | category | flops | bytes accessed | tf_op | source)
XLA Modules:
  0.0 100.8 jit_solution(12850696369914038200)
XLA Ops:
  0.6 96.6 %expert_backward.1 = (bf16[2,3072]{1,0:T(2,128)(2,1)}, bf16[168,3072]{1,0:T(8,128)(2,1)}) custom-call(bf16[2,3072]{1,0:T(2,128)(2,1)} %tok_ref.1, bf16[2,3072]{1,0:T(2,128)(2,1)} %cot_ref.1, s32[2,4]{1,0:T(2,128)} %ids_ref.1, f32[2,4]{1,0:T(2,128)} %probs_ref.1, bf16[168,3072]{1,0:T(8,128)(2,1)} %bitcast.8, bf16[168,3072]{1,0:T(8,128)(2,1)} %bitcast.9, ...), custom_call_target="tpu_custom_call" | custom-call | tf_op jit(solution)/shard_map/expert_backward/pallas_call | solution.py:537
  97.3 1.3 %copy.11 = bf16[2,3072]{1,0:T(2,128)(2,1)} copy(bf16[2,3072]{1,0:T(2,128)(2,1)} %get-tuple-element.8) | data formatting | bytes 24576
  98.6 2.2 %copy.12 = bf16[1,168,3072]{2,1,0:T(8,128)(2,1)} copy(bf16[1,168,3072]{2,1,0:T(8,128)(2,1)} %bitcast.11) | data formatting | bytes 2064384

commit v5 on v4

--- a/solution.py
+++ b/solution.py
@@ -448,12 +448,12 @@
                 push(onces[p].at[r], nears[p].at[r - 1], 6, p, b_recv.at[p],
                      grid.device(ORDERS[p][1], r))
 
-    hand_over(1)
     hand_over(0)
-    set_out(1)
     hand_over(2)
     set_out(0)
+    hand_over(1)
     set_out(2)
+    set_out(1)
     for tau in range(2, 6):
         for p in (0, 2):
             reduce_hop(p, tau // 2 + 1, tau % 2)
@@ -465,13 +465,13 @@
                 reduce_hop(1, 2, h)
     for h in range(4):
         settle(1, h)
+    for h in (0, 1):
+        for p in (0, 2):
+            settle(p, h)
     for p in range(PIECES):
         descend(p, 1)
     store = pltpu.make_async_copy(dg, dg_ref, load_sem.at[0])
     store.start()
-    for h in (0, 1):
-        for p in (0, 2):
-            settle(p, h)
 
     order = (0, 2, 1)
     for p in order:

time: 101 us -> 99.3 us (0.983)
  Pallas kernels: 96.6 us -> 94.8 us
    pallas_call x1, Pallas kernels: 96.6 us -> 94.8 us  [on_device(): pl.pallas_call(functools.partial(kernel, sizes), out_shape=(jax.ShapeDtyp...]
where the time goes in v5:
time: 99.3 us; the launch traced here: 99 us
  Pallas kernels  94.8 us (95%)
  local copies, waits for them, and re-layouts  3.56 us (4%)
    pallas_call x1, Pallas kernels, on_device(): pl.pallas_call(functools.partial(kernel, sizes), out_shape=(jax.ShapeDtyp...  94.8 us
    unnamed x2, local copies, waits for them, and re-layouts  3.56 us

profile of v5, /device:TPU:6, one launch (start us, length us, event | category | flops | bytes accessed | tf_op | source)
XLA Modules:
  0.0 99.0 jit_solution(17237679333504819189)
XLA Ops:
  0.6 94.8 %expert_backward.1 = (bf16[2,3072]{1,0:T(2,128)(2,1)}, bf16[168,3072]{1,0:T(8,128)(2,1)}) custom-call(bf16[2,3072]{1,0:T(2,128)(2,1)} %tok_ref.1, bf16[2,3072]{1,0:T(2,128)(2,1)} %cot_ref.1, s32[2,4]{1,0:T(2,128)} %ids_ref.1, f32[2,4]{1,0:T(2,128)} %probs_ref.1, bf16[168,3072]{1,0:T(8,128)(2,1)} %bitcast.8, bf16[168,3072]{1,0:T(8,128)(2,1)} %bitcast.9, ...), custom_call_target="tpu_custom_call" | custom-call | tf_op jit(solution)/shard_map/expert_backward/pallas_call | solution.py:537
  95.4 1.3 %copy.11 = bf16[2,3072]{1,0:T(2,128)(2,1)} copy(bf16[2,3072]{1,0:T(2,128)(2,1)} %get-tuple-element.8) | data formatting | bytes 24576
  96.8 2.2 %copy.12 = bf16[1,168,3072]{2,1,0:T(8,128)(2,1)} copy(bf16[1,168,3072]{2,1,0:T(8,128)(2,1)} %bitcast.11) | data formatting | bytes 2064384
